TPU v7x, 32 devices: a whole 2x2x4 slice. The times are simulated.
32 devices in a mesh: pipe: 4 (over z), ctx: 8 (over y, x, core).
Axes of the slice: x: 2, y: 2, z: 4, core: 2. Of those that a mesh axis runs over, the one named last changes fastest.
Arguments:
- queries: bfloat16 [4, 3072, 4096], P('pipe', 'ctx'), may hold values from -1.796875 to 1.796875
- key_rows: bfloat16 [4, 3072, 4096], P('pipe', 'ctx'), may hold values from -1.796875 to 1.796875
- value_rows: bfloat16 [4, 3072, 4096], P('pipe', 'ctx'), may hold values from -6 to 6
- next_grads: bfloat16 [4, 3072, 4096], P('pipe', 'ctx'), may hold values from -0.29882812 to 0.29882812
- log_decay: float32 [4, 32, 3072], P('pipe', None, 'ctx'), may hold values from -1.5 to 0, as said below
- doc_ids: int32 [4, 3072], P('pipe', 'ctx'), may hold values from 0 to 3, never falling along the last dimension, each value on 1 to 1536 neighbouring positions
- prefix_states: float32 [4, 8, 32, 128, 128], P('pipe', 'ctx'), may hold values from -24 to 24
Outputs:
- grad_q: bfloat16 [4, 3072, 4096], P('pipe', 'ctx')
- grad_k: bfloat16 [4, 3072, 4096], P('pipe', 'ctx')
- grad_v: bfloat16 [4, 3072, 4096], P('pipe', 'ctx')
Inputs may be any that keep to these rules, and one draw needn't show every extreme that they name: `doc_ids`: in each section ids never fall along the sequence; each of the 4 documents holds 1 to 1536 tokens, one exactly 1536. `log_decay`: every entry is negative.
All inputs are finite; a program needn't handle non-finite values.
Results may differ from a plain program's by a relative error of at most 0.0053.
Values may be sent and summed in bfloat16 or wider, within the bound.
A program may use at most 192 MiB of HBM per device.

v0:
```python
import jax
import jax.numpy as jnp
from jax import lax
from jax.sharding import PartitionSpec as P


def passed_along(value, axis, steps):
    count = lax.axis_size(axis)
    pairs = [(source, (source + steps) % count) for source in range(count)]
    return lax.ppermute(value, axis, pairs)


def shifted(block, axis, distance):
    devices = range(lax.axis_size(axis))
    route = [(i - distance, i) for i in devices if i - distance in devices]
    return lax.ppermute(block, axis, route)


def carried_in(part, axis, combine, identity):
    count = lax.axis_size(axis)
    place = lax.axis_index(axis)
    ahead = count - 1 - place
    gathered = jax.tree.map(lambda a: lax.all_gather(a, axis), part)
    state = jax.tree.map(lambda a, e: jnp.zeros_like(a) + jnp.asarray(e, a.dtype), part, identity)

    def one(turn, state):
        source = count - 1 - turn
        return combine(
            state, jax.tree.map(lambda a: lax.dynamic_index_in_dim(a, source, 0, False), gathered)
        )

    return lax.fori_loop(0, ahead, one, state)


def local_block(
    queries, key_rows, value_rows, grad_rows, log_decay, doc_ids, prefix_state, prior_last
):
    head_count = log_decay.shape[0]
    length = queries.shape[0]
    head_dim = queries.shape[1] // head_count
    query_heads = queries.reshape(length, head_count, head_dim)
    key_heads = key_rows.reshape(length, head_count, head_dim)
    value_heads = value_rows.reshape(length, head_count, head_dim)
    grad_heads = grad_rows.reshape(length, head_count, head_dim)
    running = jnp.cumsum(log_decay, axis=1)
    block_total = running[:, -1]
    position = lax.iota(jnp.int32, length)
    same_doc = (doc_ids[:, None] == doc_ids[None, :]) & (position[None, :] <= position[:, None])
    spread = running[:, :, None] - running[:, None, :]
    weight = jnp.where(same_doc[None], jnp.exp(jnp.where(same_doc[None], spread, 0.0)), 0.0)
    scores = jnp.einsum("ihd,jhd->hij", query_heads, key_heads, preferred_element_type=jnp.float32)
    attention = (weight * scores).astype(jnp.bfloat16)
    grad_dots = jnp.einsum(
        "ihd,jhd->hij", grad_heads, value_heads, preferred_element_type=jnp.float32
    )
    grad_mix = (weight * grad_dots).astype(jnp.bfloat16)
    continues = prior_last == doc_ids[0] + 1
    head_mask = jnp.where((doc_ids == doc_ids[0]) & continues, 1.0, 0.0)
    head_weight = jnp.exp(running).T * head_mask[:, None]
    weighted = (head_weight[:, :, None] * grad_heads).astype(jnp.bfloat16)
    head_state = jnp.einsum(
        "ihd,ihe->hde", query_heads, weighted, preferred_element_type=jnp.float32
    )
    carry_link = jnp.where((doc_ids[0] == doc_ids[-1]) & continues, jnp.exp(block_total), 0.0)
    grad_prefix = (
        jnp.einsum(
            "hde,ihe->ihd",
            prefix_state.astype(jnp.bfloat16),
            grad_heads,
            preferred_element_type=jnp.float32,
        )
        * head_weight[:, :, None]
    )
    grad_query = (
        jnp.einsum("hij,jhd->ihd", grad_mix, key_heads, preferred_element_type=jnp.float32)
        + grad_prefix
    )
    key_inner = jnp.einsum(
        "hij,ihd->jhd", grad_mix, query_heads, preferred_element_type=jnp.float32
    )
    value_inner = jnp.einsum(
        "hij,ihd->jhd", attention, grad_heads, preferred_element_type=jnp.float32
    )
    tail_mask = (doc_ids == doc_ids[-1])[None, :]
    tail_weight = jnp.where(
        tail_mask, jnp.exp(jnp.where(tail_mask, block_total[:, None] - running, 0.0)), 0.0
    ).T
    grad_query = grad_query.astype(jnp.bfloat16).reshape(length, -1)
    return (grad_query, key_inner, value_inner, head_state, carry_link, tail_weight)


def on_device(queries, key_rows, value_rows, next_grads, log_decay, doc_ids, prefix_states):
    out_grads = passed_along(next_grads, "pipe", -1)
    doc_row = doc_ids[0]
    prior_last = shifted(doc_row[-1:] + 1, "ctx", 1)
    grad_query, key_inner, value_inner, head_state, carry_link, tail_weight = local_block(
        queries[0],
        key_rows[0],
        value_rows[0],
        out_grads[0],
        log_decay[0],
        doc_row,
        prefix_states[0, 0],
        prior_last[0],
    )

    def combine(earlier_part, later_part):
        return (
            later_part[0] * earlier_part[0],
            later_part[1] + later_part[0][:, None, None] * earlier_part[1],
        )

    identity = (jnp.ones_like(carry_link), jnp.zeros_like(head_state))
    suffix = carried_in((carry_link, head_state), "ctx", combine, identity)[1]
    length = key_rows.shape[1]
    head_count = suffix.shape[0]
    head_dim = suffix.shape[1]
    key_heads = key_rows[0].reshape(length, head_count, head_dim)
    value_heads = value_rows[0].reshape(length, head_count, head_dim)
    suffix_low = suffix.astype(jnp.bfloat16)
    grad_key = (
        key_inner
        + jnp.einsum("hde,jhe->jhd", suffix_low, value_heads, preferred_element_type=jnp.float32)
        * tail_weight[:, :, None]
    )
    grad_value = (
        value_inner
        + jnp.einsum("hde,jhd->jhe", suffix_low, key_heads, preferred_element_type=jnp.float32)
        * tail_weight[:, :, None]
    )
    grad_key = grad_key.astype(jnp.bfloat16).reshape(length, -1)
    grad_value = grad_value.astype(jnp.bfloat16).reshape(length, -1)
    return (grad_query[None], grad_key[None], grad_value[None])


def solution(mesh):
    return jax.shard_map(
        on_device,
        mesh=mesh,
        in_specs=(
            P("pipe", "ctx", None),
            P("pipe", "ctx", None),
            P("pipe", "ctx", None),
            P("pipe", "ctx", None),
            P("pipe", None, "ctx"),
            P("pipe", "ctx"),
            P("pipe", "ctx", None, None, None),
        ),
        out_specs=(P("pipe", "ctx", None), P("pipe", "ctx", None), P("pipe", "ctx", None)),
        check_vma=False,
    )
```

profile of v0, /device:TPU:0, one launch (start us, length us, event | category | flops | bytes accessed | tf_op | source)
XLA Modules:
  0.0 255.8 jit_solution(7426017114410876482)
XLA Ops:
  7.2 0.0 all-gather.4.cloned.1.call-start
  7.2 4.6 %copy.65 = bf16[1,384,4096]{1,2,0:T(8,128)(2,1)} copy(bf16[1,384,4096]{2,1,0:T(8,128)(2,1)} %param.12) | data formatting | bytes 6291456 | tf_op args[3]
  11.9 5.0 %collective-permute-start = (bf16[1,384,4096]{1,2,0:T(8,128)(2,1)}, bf16[1,384,4096]{1,2,0:T(8,128)(2,1)}, u32[]{:S(2)}, u32[]{:S(2)}) collective-permute-start(bf16[1,384,4096]{1,2,0:T(8,128)(2,1)} %copy.65), channel_id=1, source_target_pairs={{0,24},{8,0},{16,8},{24,16},{1,25},{9,1},{17,9},{25,17},{2,26},{10... | collective-permute-start | bytes 9437192 | tf_op jit(solution)/shard_map/ppermute | solution.py:10
  16.9 0.0 copy-done.6
  16.9 0.6 fusion.41
  18.2 2.4 collective-permute-start.1
  22.6 0.9 reduce-window.6
  23.4 0.2 slice_reduce_fusion
  23.7 2.7 %copy.87 = bf16[48,8,32,128]{3,2,1,0:T(8,128)(2,1)S(1)} copy(bf16[48,8,32,128]{3,1,2,0:T(8,128)(2,1)} %bitcast.89) | data formatting | bytes 6291456
  26.4 0.7 compare_reduce_fusion
  27.1 0.1 copy_bitcast_fusion
  27.7 0.2 slice_reduce_fusion.1
  27.9 0.7 and_select_fusion
  28.6 0.1 select_bitcast_fusion
  28.7 55.9 %collective-permute-done = bf16[1,384,4096]{1,2,0:T(8,128)(2,1)} collective-permute-done((bf16[1,384,4096]{1,2,0:T(8,128)(2,1)}, bf16[1,384,4096]{1,2,0:T(8,128)(2,1)}, u32[]{:S(2)}, u32[]{:S(2)}) %collective-permute-start) | collective-permute-done | bytes 3145760 | tf_op jit(solution)/shard_map/ppermute | solution.py:10
  84.6 6.3 %fusion.32 = f32[32,128,128]{1,2,0:T(8,128)} fusion(bf16[384,32,128]{2,1,0:T(8,128)(2,1)S(1)} %bitcast.81, bf16[384,32,128]{0,2,1:T(8,128)(2,1)} %bitcast.2, f32[384,32]{0,1:T(8,128)S(1)} %get-tuple-element.128), kind=kOutput, calls=%fused_computation.34 | convolution fusion | flops 407371776 | bytes 8437760 | tf_op jit(solution)/shard_map/ihd,ihe->hde/dot_general | solution.py:61
  90.9 2.9 %copy.72 = f32[32,128,128]{2,1,0:T(8,128)} copy(f32[32,128,128]{1,2,0:T(8,128)} %fusion.32) | data formatting | bytes 4194304 | tf_op jit(solution)/shard_map/ihd,ihe->hde/dot_general | solution.py:61
  93.8 0.0 all-gather.4.cloned.1.call-update
  93.9 0.0 copy-start.4
  93.9 4.6 %copy.85 = bf16[48,8,32,128]{3,2,1,0:T(8,128)(2,1)} copy(bf16[48,8,32,128]{3,1,2,0:T(8,128)(2,1)} %bitcast.90) | data formatting | bytes 6291456
  98.4 0.8 copy.86
  99.3 0.7 dynamic-slice
  100.6 0.1 fusion.37
  100.8 0.2 dynamic-update-slice
  101.0 13.3 %all-reduce = f32[256]{0:T(256)S(1)} all-reduce(f32[256]{0:T(256)S(1)} %dynamic-update-slice), channel_id=3, replica_groups=mesh['pipe'=4,'ctx'=8] {'ctx'}, use_global_device_ids=true, to_apply=%add | all-reduce | flops 256 | bytes 2048
  114.3 0.1 reshape.122
  114.4 15.9 %multiply_convert_fusion.1 = bf16[32,384,384]{2,1,0:T(8,128)(2,1)} fusion(f32[32,384]{1,0:T(8,128)S(1)} %copy_bitcast_fusion, pred[384,384]{1,0:T(8,128)(4,1)S(1)} %fusion.37, bf16[384,32,128]{0,2,1:T(8,128)(2,1)} %bitcast.2, bf16[384,32,128]{2,1,0:T(8,128)(2,1)} %bitcast.85), kind=kOutput, calls=%fused_computation.3 | convolution fusion | flops 1231552512 | bytes 15925248 | tf_op jit(solution)/shard_map/ihd,jhd->hij/dot_general | solution.py:53
  130.3 10.5 %fusion.18 = f32[32,384,128]{1,2,0:T(8,128)} fusion(bf16[32,384,384]{2,1,0:T(8,128)(2,1)} %multiply_convert_fusion.1, bf16[384,32,128]{2,1,0:T(8,128)(2,1)S(1)} %bitcast.78), kind=kOutput, calls=%fused_computation.26 | convolution fusion | flops 1207959552 | bytes 18874368 | tf_op jit(solution)/shard_map/hij,jhd->ihd/dot_general | solution.py:75
  140.7 5.3 %fusion.10 = bf16[384,32,128]{0,2,1:T(8,128)(2,1)S(1)} fusion(f32[32,384,128]{1,2,0:T(8,128)} %fusion.18, f32[384,32]{0,1:T(8,128)S(1)} %get-tuple-element.128, bf16[384,32,128]{0,2,1:T(8,128)(2,1)} %bitcast.2, f32[1,1,32,128,128]{4,3,2,1,0:T(8,128)} %param.15), kind=kOutput, calls=%fused_computation.18 | convolution fusion | flops 407896064 | bytes 14729216 | tf_op jit(solution)/shard_map/hde,ihe->ihd/dot_general | solution.py:66
  146.1 2.9 %copy.78 = bf16[1,384,4096]{2,1,0:T(8,128)(2,1)} copy(bf16[1,384,4096]{1,2,0:T(8,128)(2,1)S(1)} %bitcast.87) | data formatting | bytes 6291456
  148.9 37.0 %all-gather.4.cloned.1.call-done = f32[256,128,128]{2,1,0:T(8,128)} async-done(((f32[32,128,128]{2,1,0:T(8,128)}), f32[256,128,128]{2,1,0:T(8,128)}) %all-gather.4.cloned.1.call-update) | async-done | bytes 16777232 | tf_op jit(solution)/shard_map/all_gather | solution.py:23
  185.9 0.2 broadcast_in_dim.68
  186.1 14.4 %while.14 = (s32[]{:T(128)}, f32[32,128,128]{2,1,0:T(8,128)S(1)}, s32[]{:T(128)}, f32[8,32,128,128]{3,2,1,0:T(8,128)}, f32[8,32]{1,0:T(8,128)S(1)}, /*index=5*/s32[]{:T(128)}, s32[]{:T(128)}, s32[]{:T(128)}, s32[]{:T(128)}) while((s32[]{:T(128)}, f32[32,128,128]{2,1,0:T(8,128)S(1)}, s32[]{:T(128)}, f32[8,32,128,128]{3,2,1,0:T(8,128)}, ...), condition=%wide.region_3.4_spmd, body=%wide.region_2.3_spmd.sunk | while | flops 1048582 | bytes 6291987 | solution.py:32
  186.2 2.0 bitcast_add_fusion.2
  188.2 2.0 bitcast_add_fusion.2
  190.2 2.0 bitcast_add_fusion.2
  192.2 2.0 bitcast_add_fusion.2
  194.2 2.0 bitcast_add_fusion.2
  196.3 2.0 bitcast_add_fusion.2
  198.3 2.0 bitcast_add_fusion.2
  200.5 0.0 slice-start
  200.5 0.0 slice-start.1
  200.5 7.8 %fusion.15 = f32[32,128,384]{2,1,0:T(8,128)} fusion(bf16[384,32,128]{2,1,0:T(8,128)(2,1)} %bitcast.86, f32[32,128,128]{2,1,0:T(8,128)S(1)} %get-tuple-element.87), kind=kOutput, calls=%fused_computation.23 | convolution fusion | flops 403177472 | bytes 11534336 | tf_op jit(solution)/shard_map/hde,jhe->jhd/dot_general | solution.py:123
  208.4 6.5 %fusion.20 = f32[32,128,384]{2,1,0:T(8,128)} fusion(bf16[384,32,128]{2,1,0:T(8,128)(2,1)S(1)} %bitcast.79, f32[32,128,128]{2,1,0:T(8,128)S(1)} %get-tuple-element.87), kind=kOutput, calls=%fused_computation.28 | convolution fusion | flops 403177472 | bytes 11534336 | tf_op jit(solution)/shard_map/hde,jhd->jhe/dot_general | solution.py:128
  214.9 9.8 %fusion.8 = bf16[384,32,128]{0,2,1:T(8,128)(2,1)} fusion(f32[32,128,384]{2,1,0:T(8,128)} %fusion.15, f32[384,32]{0,1:T(8,128)S(1)} %get-tuple-element.127, bf16[32,384,384]{2,1,0:T(8,128)(2,1)S(1)} %bitcast.77, bf16[384,32,128]{2,1,0:T(8,128)(2,1)} %bitcast.82), kind=kOutput, calls=%fused_computation.15 | convolution fusion | flops 1212678144 | bytes 22069248 | tf_op jit(solution)/shard_map/hij,ihd->jhd/dot_general | solution.py:78
  224.7 4.8 %copy.79 = bf16[1,384,4096]{2,1,0:T(8,128)(2,1)} copy(bf16[1,384,4096]{1,2,0:T(8,128)(2,1)} %bitcast.84) | data formatting | bytes 6291456
  229.5 14.8 %fusion.6 = bf16[384,32,128]{0,2,1:T(8,128)(2,1)} fusion(f32[32,128,384]{2,1,0:T(8,128)} %fusion.20, f32[384,32]{0,1:T(8,128)S(1)} %get-tuple-element.127, bf16[384,32,128]{0,2,1:T(8,128)(2,1)} %bitcast.2, f32[32,384]{1,0:T(8,128)S(1)} %copy_bitcast_fusion, pred[384,384]{1,0:T(8,128)(4,1)S(1)} %fusion.37, bf16[384,32,128]{2,1,0:T(8,128)(2,1)S(1)} %bitcast.80, ...), kind=kOutput, calls=%fused_computation.12 | convolution fusion | flops 2444230656 | bytes 19120128 | tf_op jit(solution)/shard_map/hij,ihd->jhd/dot_general | solution.py:81
  244.4 4.6 %copy.80 = bf16[1,384,4096]{2,1,0:T(8,128)(2,1)} copy(bf16[1,384,4096]{1,2,0:T(8,128)(2,1)} %bitcast.92) | data formatting | bytes 6291456
  (32 shorter events, 0.2 us)
Async XLA Ops:
  7.2 9.8 %copy-start.6 = (s32[1,384]{1,0:T(1,128)S(1)}, s32[1,384]{1,0:T(1,128)}, u32[]{:S(2)}) copy-start(s32[1,384]{1,0:T(1,128)} %param.14) | copy-start | bytes 4612
  7.2 15.3 %copy-start.5 = (f32[1,32,384]{2,1,0:T(8,128)S(1)}, f32[1,32,384]{2,1,0:T(8,128)}, u32[]{:S(2)}) copy-start(f32[1,32,384]{2,1,0:T(8,128)} %param.13) | copy-start | bytes 147460
  7.2 178.7 %all-gather.4.cloned.1.call-start = ((), (), s32[]{:S(2)}) async-start(), calls=%async_computation | async-start | bytes 18874368 | tf_op jit(solution)/shard_map/all_gather | solution.py:23
  11.9 72.7 %collective-permute-start = (bf16[1,384,4096]{1,2,0:T(8,128)(2,1)}, bf16[1,384,4096]{1,2,0:T(8,128)(2,1)}, u32[]{:S(2)}, u32[]{:S(2)}) collective-permute-start(bf16[1,384,4096]{1,2,0:T(8,128)(2,1)} %copy.65), channel_id=1, source_target_pairs={{0,24},{8,0},{16,8},{24,16},{1,25},{9,1},{17,9},{25,17},{2,26},{10... | collective-permute-start | bytes 9437192 | tf_op jit(solution)/shard_map/ppermute | solution.py:10
  18.2 9.0 %collective-permute-start.1 = (s32[1]{0:T(128)}, s32[1]{0:T(128)}, u32[]{:S(2)}, u32[]{:S(2)}) collective-permute-start(s32[1]{0:T(128)} %bitcast.7), channel_id=1, source_target_pairs={{0,1},{1,2},{2,3},{3,4},{4,5},{5,6},{6,7},{8,9},{9,10},{10,11},{11... | collective-permute-start | bytes 20 | tf_op jit(solution)/shard_map/ppermute | solution.py:16
  26.4 64.6 %copy-start.3 = (bf16[48,8,32,128]{3,2,1,0:T(8,128)(2,1)}, bf16[48,8,32,128]{3,2,1,0:T(8,128)(2,1)S(1)}, u32[]{:S(2)}) copy-start(bf16[48,8,32,128]{3,2,1,0:T(8,128)(2,1)S(1)} %copy.87) | copy-start | bytes 9437188
  93.9 4.6 %copy-start.4 = (bf16[1,384,4096]{2,1,0:T(8,128)(2,1)S(1)}, bf16[1,384,4096]{2,1,0:T(8,128)(2,1)}, u32[]{:S(2)}) copy-start(bf16[1,384,4096]{2,1,0:T(8,128)(2,1)} %param.10) | copy-start | bytes 9437188
  98.4 0.8 copy-start.7
  99.3 31.0 %copy-start = (bf16[48,8,32,128]{3,2,1,0:T(8,128)(2,1)}, bf16[48,8,32,128]{3,2,1,0:T(8,128)(2,1)S(1)}, u32[]{:S(2)}) copy-start(bf16[48,8,32,128]{3,2,1,0:T(8,128)(2,1)S(1)} %copy.86) | copy-start | bytes 9437188
  200.5 7.9 %copy-start.1 = (bf16[48,8,32,128]{3,2,1,0:T(8,128)(2,1)S(1)}, bf16[48,8,32,128]{3,2,1,0:T(8,128)(2,1)}, u32[]{:S(2)}) copy-start(bf16[48,8,32,128]{3,2,1,0:T(8,128)(2,1)} %copy-done) | copy-start | bytes 9437188
  200.5 14.3 %slice-start = ((s8[9437184]{0:T(1024)(128)(4,1)}), s8[4194304]{0:T(1024)(128)(4,1)S(1)}, s32[]{:S(2)}) async-start(s8[9437184]{0:T(1024)(128)(4,1)} %bitcast.76), calls=%async_computation.1 | async-start | bytes 8388608
  200.5 14.3 %slice-start.1 = ((s8[9437184]{0:T(1024)(128)(4,1)}), s8[4194304]{0:T(1024)(128)(4,1)S(1)}, s32[]{:S(2)}) async-start(s8[9437184]{0:T(1024)(128)(4,1)} %bitcast.76), calls=%async_computation.2 | async-start | bytes 8388608
  208.4 6.5 %slice-start.2 = ((s8[9437184]{0:T(1024)(128)(4,1)}), s8[1048576]{0:T(1024)(128)(4,1)S(1)}, s32[]{:S(2)}) async-start(s8[9437184]{0:T(1024)(128)(4,1)} %bitcast.76), calls=%async_computation.3 | async-start | bytes 2097152
  224.7 4.8 %copy-start.2 = (bf16[48,8,32,128]{3,2,1,0:T(8,128)(2,1)S(1)}, bf16[48,8,32,128]{3,2,1,0:T(8,128)(2,1)}, u32[]{:S(2)}) copy-start(bf16[48,8,32,128]{3,2,1,0:T(8,128)(2,1)} %copy-done) | copy-start | bytes 9437188
Sparse Core Ops, SparseCore 0:
  94.0 91.8 all-gather.3
where the time goes:
time: 257 us; the launch traced here: 256 us
  waiting for transfers between devices  92.9 us (36%)
  matrix products  77 us (30%)
  local copies, waits for them, and re-layouts  30 us (12%)
  between operations  18.1 us (7%)
  other arithmetic  16.6 us (6%)
  blocking collectives  13.3 us (5%)
  starting transfers between devices  7.49 us (3%)
    ppermute x1, waiting for transfers between devices, passed_along(): return lax.ppermute(value, axis, pairs)  55.9 us
    all_gather x1, waiting for transfers between devices, carried_in(): gathered = jax.tree.map(lambda a: lax.all_gather(a, axis), part)  37 us
    unnamed x32, local copies, waits for them, and re-layouts  26 us
    dot_general x1, matrix products, local_block(): jnp.einsum('ihd,jhd->hij', grad_heads, value_heads, preferred_element_typ...  15.9 us
    dot_general x1, matrix products, local_block(): jnp.einsum('hij,ihd->jhd', attention, grad_heads, preferred_element_type=...  14.8 us
    add x7, other arithmetic, combine(): later_part[1] + later_part[0][:, None, None] * earlier_part[1]  13.8 us
    unnamed x1, blocking collectives  13.3 us
    dot_general x1, matrix products, local_block(): jnp.einsum('hij,jhd->ihd', grad_mix, key_heads, preferred_element_type=jn...  10.5 us
  transfers between devices with their start and end apart: 3, of which 2 were waited for; matrix products, arithmetic and copies ran while one was open for 18% of the time, Pallas kernels for 0%

commit v1 on v0

v1 whole, which is shorter than its diff:
```python
import functools

import jax
import jax.numpy as jnp
from jax import lax
from jax.experimental import pallas as pl
from jax.experimental.pallas import tpu as pltpu
from jax.sharding import PartitionSpec as P

MESH = pl.DeviceIdType.MESH
LANES = 128
CHUNK_HEADS = 2
IN_FLIGHT = 4
MASKED = -1e30


def dot(a, b, a_dim, b_dim, precision=None):
    return lax.dot_general(
        a,
        b,
        (((a_dim,), (b_dim,)), ((), ())),
        precision=precision,
        preferred_element_type=jnp.float32,
    )


def as_columns(row, width):
    return jnp.broadcast_to(row, (width, row.shape[1])).T


def kernel(
    pipe_count,
    ctx_count,
    q_hbm,
    k_hbm,
    v_hbm,
    g_hbm,
    decay_ref,
    doc_ref,
    prefix_hbm,
    out_q,
    out_k,
    out_v,
    q_s,
    k_s,
    v_s,
    g_s,
    prefix_s,
    run_s,
    col_s,
    bias_s,
    head_mask_s,
    tail_mask_s,
    meta_own,
    meta_all,
    link_s,
    cont_s,
    state_s,
    odd_state_s,
    pair_s,
    pair_in_s,
    odd_suffix_s,
    suffix_in_s,
    load_sem,
    prefix_sem,
    store_sem,
    g_send,
    g_recv,
    meta_send,
    meta_recv,
    state_send,
    state_recv,
    pair_send,
    pair_recv,
    suffix_send,
    suffix_recv,
):
    chunks, length, chunk_cols = q_s.shape
    head_dim = chunk_cols // CHUNK_HEADS
    heads = run_s.shape[0]
    blocks = length // LANES
    pairs = ctx_count // 2
    reach = ctx_count // 4
    section = lax.axis_index("pipe")
    me = lax.axis_index("ctx")
    odd = lax.rem(me, 2)
    pair = me // 2
    earlier = lax.rem(section + pipe_count - 1, pipe_count)
    later = lax.rem(section + 1, pipe_count)

    barrier = pltpu.get_barrier_semaphore()
    pl.semaphore_signal(barrier, inc=1, device_id={"pipe": earlier}, device_id_type=MESH)
    pl.semaphore_signal(barrier, inc=1, device_id={"pipe": later}, device_id_type=MESH)
    for k in range(1, ctx_count):
        pl.semaphore_signal(
            barrier, inc=1, device_id={"ctx": lax.rem(me + k, ctx_count)}, device_id_type=MESH
        )
    pl.semaphore_wait(barrier, ctx_count + 1)

    def columns(t):
        return pl.ds(pl.multiple_of(t * chunk_cols, chunk_cols), chunk_cols)

    def grad_copy(t):
        return pltpu.make_async_remote_copy(
            src_ref=g_hbm.at[0, :, columns(t)],
            dst_ref=g_s.at[t],
            send_sem=g_send.at[t],
            recv_sem=g_recv.at[t],
            device_id={"pipe": earlier},
            device_id_type=MESH,
        )

    def load_copy(i, t):
        source, target = ((q_hbm, q_s), (k_hbm, k_s), (v_hbm, v_s))[i]
        return pltpu.make_async_copy(
            source.at[0, :, columns(t)], target.at[t], load_sem.at[i, t]
        )

    def store_copy(i, t):
        source, target = ((q_s, out_q), (k_s, out_k), (v_s, out_v))[i]
        return pltpu.make_async_copy(
            source.at[t], target.at[0, :, columns(t)], store_sem.at[i, t]
        )

    def meta_copy(k):
        return pltpu.make_async_remote_copy(
            src_ref=meta_own,
            dst_ref=meta_all.at[me],
            send_sem=meta_send.at[k],
            recv_sem=meta_recv.at[k],
            device_id={"ctx": lax.rem(me + k, ctx_count)},
            device_id_type=MESH,
        )

    def meta_arrival(k):
        return pltpu.make_async_remote_copy(
            src_ref=meta_own,
            dst_ref=meta_all.at[lax.rem(me + ctx_count - k, ctx_count)],
            send_sem=meta_send.at[k],
            recv_sem=meta_recv.at[k],
            device_id={"ctx": lax.rem(me + k, ctx_count)},
            device_id_type=MESH,
        )

    partner = me + 1 - 2 * odd

    def state_copy(t):
        return pltpu.make_async_remote_copy(
            src_ref=state_s.at[t],
            dst_ref=odd_state_s.at[t],
            send_sem=state_send.at[t],
            recv_sem=state_recv.at[t],
            device_id={"ctx": partner},
            device_id_type=MESH,
        )

    def suffix_copy(t):
        return pltpu.make_async_remote_copy(
            src_ref=odd_suffix_s.at[t],
            dst_ref=suffix_in_s.at[t],
            send_sem=suffix_send.at[t],
            recv_sem=suffix_recv.at[t],
            device_id={"ctx": partner},
            device_id_type=MESH,
        )

    def pair_copy(d, t):
        return pltpu.make_async_remote_copy(
            src_ref=pair_s.at[t],
            dst_ref=pair_in_s.at[d - 1, t],
            send_sem=pair_send.at[d - 1, t],
            recv_sem=pair_recv.at[d - 1, t],
            device_id={"ctx": lax.rem(me - 2 * d + 1 + ctx_count, ctx_count)},
            device_id_type=MESH,
        )

    for t in range(IN_FLIGHT):
        grad_copy(t).start()

    @pl.loop(0, chunks)
    def _(t):
        for i in range(3):
            load_copy(i, t).start()

    prefix_copy = pltpu.make_async_copy(prefix_hbm.at[0, 0], prefix_s, prefix_sem)
    prefix_copy.start()

    rows = lax.broadcasted_iota(jnp.int32, (length, length), 0)
    cols = lax.broadcasted_iota(jnp.int32, (length, length), 1)
    ordered = rows <= cols
    running = dot(
        decay_ref[0], jnp.where(ordered, 1.0, 0.0), 1, 0, precision=lax.Precision.HIGHEST
    )
    run_s[...] = running
    doc_row = doc_ref[...].astype(jnp.float32)
    first_doc = jnp.broadcast_to(doc_row[:, 0:1], (8, LANES))
    last_doc = jnp.broadcast_to(doc_row[:, length - 1 : length], (8, LANES))
    meta_own[0:heads] = jnp.broadcast_to(
        jnp.exp(running[:, length - 1 : length]), (heads, LANES)
    )
    meta_own[heads : heads + 8] = first_doc
    meta_own[heads + 8 : heads + 16] = last_doc
    meta_all[me] = meta_own[...]
    for k in range(1, ctx_count):
        meta_copy(k).start()

    doc_cols = as_columns(doc_row, LANES)
    doc_wide = jnp.concatenate([doc_cols] * blocks, axis=1)
    bias_s[...] = jnp.where(ordered & (doc_wide == doc_row), 0.0, MASKED)
    tail_mask_s[...] = jnp.where(doc_cols == last_doc[0:1], 1.0, 0.0)

    @pl.loop(0, heads)
    def _(h):
        col_s[h] = as_columns(run_s[pl.ds(h, 1), :], LANES)

    for k in range(1, ctx_count):
        meta_arrival(k).wait_recv()
    for b in range(ctx_count):
        first_here = meta_all[b, heads : heads + 8]
        last_here = meta_all[b, heads + 8 : heads + 16]
        if b > 0:
            last_before = meta_all[b - 1, heads + 8 : heads + 16]
            continues = jnp.where(first_here == last_before, 1.0, 0.0)
        else:
            continues = jnp.zeros((8, LANES), jnp.float32)
        cont_s[b] = continues
        passes = jnp.where(first_here == last_here, continues, 0.0)
        link_s[b] = meta_all[b, 0:heads] * passes[0:1]
    head_mask_s[...] = jnp.where(doc_cols == first_doc[0:1], 1.0, 0.0) * cont_s[me][0:1]
    prefix_copy.wait()

    def part(u):
        return slice(u * head_dim, (u + 1) * head_dim)

    def head_weight(h):
        return jnp.exp(col_s[h]) * head_mask_s[...]

    def stage_state(t):
        grad_copy(t).wait_recv()
        load_copy(0, t).wait()
        for u in range(CHUNK_HEADS):
            weighted = head_weight(t * CHUNK_HEADS + u) * g_s[t, :, part(u)].astype(jnp.float32)
            state_s[t, u] = dot(q_s[t, :, part(u)], weighted.astype(jnp.bfloat16), 0, 0)

        @pl.when(odd == 1)
        def _():
            state_copy(t).start()

        grad_copy(t).wait_send()

        @pl.when(t + IN_FLIGHT < chunks)
        def _():
            grad_copy(t + IN_FLIGHT).start()

    def stage_pair(t):
        state_copy(t).wait_recv()
        for u in range(CHUNK_HEADS):
            link = link_s[me, pl.ds(t * CHUNK_HEADS + u, 1), :]
            pair_s[t, u] = state_s[t, u] + link * odd_state_s[t, u]
        for d in range(1, reach + 1):

            @pl.when(pair >= d)
            def _():
                pair_copy(d, t).start()

    def stage_suffix(t):
        odd_suffix_s[t] = jnp.zeros(odd_suffix_s.shape[1:], jnp.float32)
        for d in range(1, reach + 1):

            @pl.when(pair + d < pairs)
            def _():
                pair_copy(d, t).wait_recv()
                for u in range(CHUNK_HEADS):
                    term = pair_in_s[d - 1, t, u]
                    for b in range(1, 2 * d - 1):
                        term = term * link_s[me + b, pl.ds(t * CHUNK_HEADS + u, 1), :]
                    odd_suffix_s[t, u] += term

        suffix_copy(t).start()

    def stage_grads(t):
        load_copy(1, t).wait()
        load_copy(2, t).wait()

        @pl.when(odd == 0)
        def _():
            suffix_copy(t).wait_recv()
            for u in range(CHUNK_HEADS):
                link = link_s[me + 1, pl.ds(t * CHUNK_HEADS + u, 1), :]
                odd_suffix_s[t, u] = odd_state_s[t, u] + link * suffix_in_s[t, u]

        for u in range(CHUNK_HEADS):
            h = t * CHUNK_HEADS + u
            q, k, v, g = (ref[t, :, part(u)] for ref in (q_s, k_s, v_s, g_s))
            suffix = odd_suffix_s[t, u].astype(jnp.bfloat16)
            prefix = prefix_s[h].astype(jnp.bfloat16)
            grad_q = [None] * blocks
            total = col_s[h, length - 1 : length, :]
            row = run_s[pl.ds(h, 1), :]
            for block in range(blocks):
                low, high = block * LANES, (block + 1) * LANES
                col = col_s[h, low:high, :]
                wide = jnp.concatenate([col] * (blocks - block), axis=1)
                weight = jnp.exp((row[:, low:] - wide) + bias_s[low:high, low:])
                scores = dot(k[low:high], q[low:], 1, 1)
                grad_dots = dot(v[low:high], g[low:], 1, 1)
                attention = (weight * scores).astype(jnp.bfloat16)
                grad_mix = (weight * grad_dots).astype(jnp.bfloat16)
                tail = jnp.exp(total - col) * tail_mask_s[low:high]
                grad_k = dot(grad_mix, q[low:], 1, 0) + dot(v[low:high], suffix, 1, 1) * tail
                grad_v = dot(attention, g[low:], 1, 0) + dot(k[low:high], suffix, 1, 0) * tail
                spread = dot(grad_mix, k[low:high], 0, 0)
                for i in range(block, blocks):
                    piece = spread[(i - block) * LANES : (i - block + 1) * LANES]
                    grad_q[i] = piece if grad_q[i] is None else grad_q[i] + piece
                k_s[t, low:high, part(u)] = grad_k.astype(jnp.bfloat16)
                v_s[t, low:high, part(u)] = grad_v.astype(jnp.bfloat16)
            grad_q = jnp.concatenate(grad_q, axis=0) + dot(g, prefix, 1, 1) * head_weight(h)
            q_s[t, :, part(u)] = grad_q.astype(jnp.bfloat16)
        for i in range(3):
            store_copy(i, t).start()

    @pl.loop(0, chunks + 3)
    def _(step):
        @pl.when(step < chunks)
        def _():
            stage_state(step)

        @pl.when((step >= 1) & (step < chunks + 1) & (odd == 0))
        def _():
            stage_pair(step - 1)

        @pl.when((step >= 2) & (step < chunks + 2) & (odd == 1))
        def _():
            stage_suffix(step - 2)

        @pl.when(step >= 3)
        def _():
            stage_grads(step - 3)

    for k in range(1, ctx_count):
        meta_copy(k).wait_send()

    @pl.loop(0, chunks)
    def _(t):
        for i in range(3):
            store_copy(i, t).wait()

        @pl.when(odd == 1)
        def _():
            state_copy(t).wait_send()
            suffix_copy(t).wait_send()

        for d in range(1, reach + 1):

            @pl.when((odd == 0) & (pair >= d))
            def _():
                pair_copy(d, t).wait_send()


def solution(mesh):
    pipe_count, ctx_count = mesh.shape["pipe"], mesh.shape["ctx"]

    def on_device(queries, key_rows, value_rows, next_grads, log_decay, doc_ids, prefix_states):
        _, length, width = queries.shape
        heads = log_decay.shape[1]
        head_dim = width // heads
        chunks = heads // CHUNK_HEADS
        chunk_cols = head_dim * CHUNK_HEADS
        reach = ctx_count // 4
        any_spec = pl.BlockSpec(memory_space=pl.ANY)
        vmem_spec = pl.BlockSpec(memory_space=pltpu.VMEM)
        f32, bf16 = jnp.float32, jnp.bfloat16
        rows = pltpu.VMEM((chunks, length, chunk_cols), bf16)
        states = pltpu.VMEM((chunks, CHUNK_HEADS, head_dim, head_dim), f32)
        mask = pltpu.VMEM((length, LANES), f32)
        dma = pltpu.SemaphoreType.DMA
        return pl.pallas_call(
            functools.partial(kernel, pipe_count, ctx_count),
            out_shape=[jax.ShapeDtypeStruct(queries.shape, bf16)] * 3,
            in_specs=[any_spec] * 4 + [vmem_spec] * 2 + [any_spec],
            out_specs=[any_spec] * 3,
            scratch_shapes=[
                rows,
                rows,
                rows,
                rows,
                pltpu.VMEM((heads, head_dim, head_dim), f32),
                pltpu.VMEM((heads, length), f32),
                pltpu.VMEM((heads, length, LANES), f32),
                pltpu.VMEM((length, length), f32),
                mask,
                mask,
                pltpu.VMEM((heads + 16, LANES), f32),
                pltpu.VMEM((ctx_count, heads + 16, LANES), f32),
                pltpu.VMEM((ctx_count, heads, LANES), f32),
                pltpu.VMEM((ctx_count, 8, LANES), f32),
                states,
                states,
                states,
                pltpu.VMEM((reach, chunks, CHUNK_HEADS, head_dim, head_dim), f32),
                states,
                states,
                dma((3, chunks)),
                dma,
                dma((3, chunks)),
                dma((chunks,)),
                dma((chunks,)),
                dma((ctx_count,)),
                dma((ctx_count,)),
                dma((chunks,)),
                dma((chunks,)),
                dma((reach, chunks)),
                dma((reach, chunks)),
                dma((chunks,)),
                dma((chunks,)),
            ],
            compiler_params=pltpu.CompilerParams(
                collective_id=0, has_side_effects=True, vmem_limit_bytes=56 * 1024 * 1024
            ),
        )(queries, key_rows, value_rows, next_grads, log_decay, doc_ids, prefix_states)

    return jax.shard_map(
        on_device,
        mesh=mesh,
        in_specs=(
            P("pipe", "ctx", None),
            P("pipe", "ctx", None),
            P("pipe", "ctx", None),
            P("pipe", "ctx", None),
            P("pipe", None, "ctx"),
            P("pipe", "ctx"),
            P("pipe", "ctx", None, None, None),
        ),
        out_specs=(P("pipe", "ctx", None), P("pipe", "ctx", None), P("pipe", "ctx", None)),
        check_vma=False,
    )
```

time: 257 us -> 97.5 us (0.38)
  the two profiles are of different devices: /device:TPU:0 before, /device:TPU:27 now
where the time goes in v1:
time: 97.5 us; the launch traced here: 97.3 us
  Pallas kernels  87.9 us (90%)
  local copies, waits for them, and re-layouts  8.75 us (9%)
    pallas_call x1, Pallas kernels, on_device(): pl.pallas_call(functools.partial(kernel, pipe_count, ctx_count), out_shap...  87.9 us
    unnamed x7, local copies, waits for them, and re-layouts  8.75 us

profile of v1, /device:TPU:27, one launch (start us, length us, event | category | flops | bytes accessed | tf_op | source)
XLA Modules:
  0.0 97.3 jit_solution(9658341634248063820)
XLA Ops:
  0.6 87.9 %shard_map.94 = (bf16[1,384,4096]{2,1,0:T(8,128)(2,1)}, bf16[1,384,4096]{2,1,0:T(8,128)(2,1)}, bf16[1,384,4096]{2,1,0:T(8,128)(2,1)}) custom-call(bf16[1,384,4096]{2,1,0:T(8,128)(2,1)} %q_hbm.1, bf16[1,384,4096]{2,1,0:T(8,128)(2,1)} %k_hbm.1, bf16[1,384,4096]{2,1,0:T(8,128)(2,1)} %v_hbm.1, bf16[1,384,4096]{2,1,0:T(8,128)(2,1)} %g_hbm.1, ...), custom_call_target="tpu_custom_call" | custom-call | tf_op jit(solution)/shard_map/pallas_call | solution.py:378
  88.6 0.0 copy-start.1
  88.6 4.1 %copy.13 = bf16[1,384,4096]{2,1,0:T(8,128)(2,1)} copy(bf16[1,384,4096]{2,1,0:T(8,128)(2,1)} %get-tuple-element.6) | data formatting | bytes 6291456
  92.6 0.0 copy-done.1
  92.6 0.0 copy-start
  92.6 1.7 %copy.14 = bf16[1,384,4096]{2,1,0:T(8,128)(2,1)} copy(bf16[1,384,4096]{2,1,0:T(8,128)(2,1)S(1)} %copy-done.1) | data formatting | bytes 6291456
  94.3 1.4 %copy-done = bf16[1,384,4096]{2,1,0:T(8,128)(2,1)S(1)} copy-done((bf16[1,384,4096]{2,1,0:T(8,128)(2,1)S(1)}, bf16[1,384,4096]{2,1,0:T(8,128)(2,1)}, u32[]{:S(2)}) %copy-start) | copy-done | bytes 3145752
  95.7 1.7 %copy.15 = bf16[1,384,4096]{2,1,0:T(8,128)(2,1)} copy(bf16[1,384,4096]{2,1,0:T(8,128)(2,1)S(1)} %copy-done) | data formatting | bytes 6291456
Async XLA Ops:
  88.6 4.1 %copy-start.1 = (bf16[1,384,4096]{2,1,0:T(8,128)(2,1)S(1)}, bf16[1,384,4096]{2,1,0:T(8,128)(2,1)}, u32[]{:S(2)}) copy-start(bf16[1,384,4096]{2,1,0:T(8,128)(2,1)} %get-tuple-element.7) | copy-start | bytes 9437188
  92.6 3.0 %copy-start = (bf16[1,384,4096]{2,1,0:T(8,128)(2,1)S(1)}, bf16[1,384,4096]{2,1,0:T(8,128)(2,1)}, u32[]{:S(2)}) copy-start(bf16[1,384,4096]{2,1,0:T(8,128)(2,1)} %get-tuple-element.8) | copy-start | bytes 9437188

commit v2 on v1

--- a/solution.py
+++ b/solution.py
@@ -11,6 +11,7 @@
 LANES = 128
 CHUNK_HEADS = 2
 IN_FLIGHT = 4
+SLOTS = 3
 MASKED = -1e30
 
 
@@ -61,9 +62,9 @@
     pair_in_s,
     odd_suffix_s,
     suffix_in_s,
+    inner_s,
     load_sem,
     prefix_sem,
-    store_sem,
     g_send,
     g_recv,
     meta_send,
@@ -116,12 +117,6 @@
             source.at[0, :, columns(t)], target.at[t], load_sem.at[i, t]
         )
 
-    def store_copy(i, t):
-        source, target = ((q_s, out_q), (k_s, out_k), (v_s, out_v))[i]
-        return pltpu.make_async_copy(
-            source.at[t], target.at[0, :, columns(t)], store_sem.at[i, t]
-        )
-
     def meta_copy(k):
         return pltpu.make_async_remote_copy(
             src_ref=meta_own,
@@ -278,9 +273,32 @@
 
         suffix_copy(t).start()
 
-    def stage_grads(t):
-        load_copy(1, t).wait()
-        load_copy(2, t).wait()
+    def stage_inner(t, u):
+        h = t * CHUNK_HEADS + u
+        slot = lax.rem(t, SLOTS)
+        q, k, v, g = (ref[t, :, part(u)] for ref in (q_s, k_s, v_s, g_s))
+        row = run_s[pl.ds(h, 1), :]
+        grad_q = [None] * blocks
+        for block in range(blocks):
+            low, high = block * LANES, (block + 1) * LANES
+            wide = jnp.concatenate([col_s[h, low:high, :]] * (blocks - block), axis=1)
+            weight = jnp.exp((row[:, low:] - wide) + bias_s[low:high, low:])
+            scores = dot(k[low:high], q[low:], 1, 1)
+            grad_dots = dot(v[low:high], g[low:], 1, 1)
+            attention = (weight * scores).astype(jnp.bfloat16)
+            grad_mix = (weight * grad_dots).astype(jnp.bfloat16)
+            inner_s[slot, 0, low:high, part(u)] = dot(grad_mix, q[low:], 1, 0)
+            inner_s[slot, 1, low:high, part(u)] = dot(attention, g[low:], 1, 0)
+            spread = dot(grad_mix, k[low:high], 0, 0)
+            for i in range(block, blocks):
+                piece = spread[(i - block) * LANES : (i - block + 1) * LANES]
+                grad_q[i] = piece if grad_q[i] is None else grad_q[i] + piece
+        prefix = prefix_s[h].astype(jnp.bfloat16)
+        grad_q = jnp.concatenate(grad_q, axis=0) + dot(g, prefix, 1, 1) * head_weight(h)
+        out_q[t, :, part(u)] = grad_q.astype(jnp.bfloat16)
+
+    def stage_finish(t):
+        slot = lax.rem(t, SLOTS)
 
         @pl.when(odd == 0)
         def _():
@@ -291,61 +309,44 @@
 
         for u in range(CHUNK_HEADS):
             h = t * CHUNK_HEADS + u
-            q, k, v, g = (ref[t, :, part(u)] for ref in (q_s, k_s, v_s, g_s))
             suffix = odd_suffix_s[t, u].astype(jnp.bfloat16)
-            prefix = prefix_s[h].astype(jnp.bfloat16)
-            grad_q = [None] * blocks
-            total = col_s[h, length - 1 : length, :]
-            row = run_s[pl.ds(h, 1), :]
-            for block in range(blocks):
-                low, high = block * LANES, (block + 1) * LANES
-                col = col_s[h, low:high, :]
-                wide = jnp.concatenate([col] * (blocks - block), axis=1)
-                weight = jnp.exp((row[:, low:] - wide) + bias_s[low:high, low:])
-                scores = dot(k[low:high], q[low:], 1, 1)
-                grad_dots = dot(v[low:high], g[low:], 1, 1)
-                attention = (weight * scores).astype(jnp.bfloat16)
-                grad_mix = (weight * grad_dots).astype(jnp.bfloat16)
-                tail = jnp.exp(total - col) * tail_mask_s[low:high]
-                grad_k = dot(grad_mix, q[low:], 1, 0) + dot(v[low:high], suffix, 1, 1) * tail
-                grad_v = dot(attention, g[low:], 1, 0) + dot(k[low:high], suffix, 1, 0) * tail
-                spread = dot(grad_mix, k[low:high], 0, 0)
-                for i in range(block, blocks):
-                    piece = spread[(i - block) * LANES : (i - block + 1) * LANES]
-                    grad_q[i] = piece if grad_q[i] is None else grad_q[i] + piece
-                k_s[t, low:high, part(u)] = grad_k.astype(jnp.bfloat16)
-                v_s[t, low:high, part(u)] = grad_v.astype(jnp.bfloat16)
-            grad_q = jnp.concatenate(grad_q, axis=0) + dot(g, prefix, 1, 1) * head_weight(h)
-            q_s[t, :, part(u)] = grad_q.astype(jnp.bfloat16)
-        for i in range(3):
-            store_copy(i, t).start()
-
-    @pl.loop(0, chunks + 3)
+            tail = jnp.exp(col_s[h, length - 1 : length, :] - col_s[h]) * tail_mask_s[...]
+            grad_k = inner_s[slot, 0, :, part(u)] + dot(v_s[t, :, part(u)], suffix, 1, 1) * tail
+            grad_v = inner_s[slot, 1, :, part(u)] + dot(k_s[t, :, part(u)], suffix, 1, 0) * tail
+            out_k[t, :, part(u)] = grad_k.astype(jnp.bfloat16)
+            out_v[t, :, part(u)] = grad_v.astype(jnp.bfloat16)
+
+    @pl.loop(0, chunks + 2)
     def _(step):
         @pl.when(step < chunks)
         def _():
             stage_state(step)
-
-        @pl.when((step >= 1) & (step < chunks + 1) & (odd == 0))
-        def _():
-            stage_pair(step - 1)
-
-        @pl.when((step >= 2) & (step < chunks + 2) & (odd == 1))
-        def _():
-            stage_suffix(step - 2)
-
-        @pl.when(step >= 3)
-        def _():
-            stage_grads(step - 3)
+            load_copy(1, step).wait()
+            load_copy(2, step).wait()
+            for u in range(CHUNK_HEADS - 1):
+                stage_inner(step, u)
+
+        @pl.when((step < chunks) & (odd == 0))
+        def _():
+            stage_pair(step)
+
+        @pl.when(step < chunks)
+        def _():
+            stage_inner(step, CHUNK_HEADS - 1)
+
+        @pl.when((step >= 1) & (step < chunks + 1) & (odd == 1))
+        def _():
+            stage_suffix(step - 1)
+
+        @pl.when(step >= 2)
+        def _():
+            stage_finish(step - 2)
 
     for k in range(1, ctx_count):
         meta_copy(k).wait_send()
 
     @pl.loop(0, chunks)
     def _(t):
-        for i in range(3):
-            store_copy(i, t).wait()
-
         @pl.when(odd == 1)
         def _():
             state_copy(t).wait_send()
@@ -356,6 +357,21 @@
             @pl.when((odd == 0) & (pair >= d))
             def _():
                 pair_copy(d, t).wait_send()
+
+
+def place_kernel(in_q, in_k, in_v, out_q, out_k, out_v, sem):
+    chunks, _, chunk_cols = in_q.shape
+    copies = [
+        pltpu.make_async_copy(
+            source.at[t], target.at[0, :, t * chunk_cols : (t + 1) * chunk_cols], sem.at[i, t]
+        )
+        for i, (source, target) in enumerate(((in_q, out_q), (in_k, out_k), (in_v, out_v)))
+        for t in range(chunks)
+    ]
+    for copy in copies:
+        copy.start()
+    for copy in copies:
+        copy.wait()
 
 
 def solution(mesh):
@@ -375,11 +391,11 @@
         states = pltpu.VMEM((chunks, CHUNK_HEADS, head_dim, head_dim), f32)
         mask = pltpu.VMEM((length, LANES), f32)
         dma = pltpu.SemaphoreType.DMA
-        return pl.pallas_call(
+        grads = pl.pallas_call(
             functools.partial(kernel, pipe_count, ctx_count),
-            out_shape=[jax.ShapeDtypeStruct(queries.shape, bf16)] * 3,
+            out_shape=[pltpu.VMEM((chunks, length, chunk_cols), bf16)] * 3,
             in_specs=[any_spec] * 4 + [vmem_spec] * 2 + [any_spec],
-            out_specs=[any_spec] * 3,
+            out_specs=[vmem_spec] * 3,
             scratch_shapes=[
                 rows,
                 rows,
@@ -401,9 +417,9 @@
                 pltpu.VMEM((reach, chunks, CHUNK_HEADS, head_dim, head_dim), f32),
                 states,
                 states,
+                pltpu.VMEM((SLOTS, 2, length, chunk_cols), f32),
                 dma((3, chunks)),
                 dma,
-                dma((3, chunks)),
                 dma((chunks,)),
                 dma((chunks,)),
                 dma((ctx_count,)),
@@ -416,9 +432,17 @@
                 dma((chunks,)),
             ],
             compiler_params=pltpu.CompilerParams(
-                collective_id=0, has_side_effects=True, vmem_limit_bytes=56 * 1024 * 1024
+                collective_id=0, has_side_effects=True, vmem_limit_bytes=50 * 1024 * 1024
             ),
         )(queries, key_rows, value_rows, next_grads, log_decay, doc_ids, prefix_states)
+        return pl.pallas_call(
+            place_kernel,
+            out_shape=[jax.ShapeDtypeStruct(queries.shape, bf16)] * 3,
+            in_specs=[vmem_spec] * 3,
+            out_specs=[any_spec] * 3,
+            scratch_shapes=[dma((3, chunks))],
+            compiler_params=pltpu.CompilerParams(vmem_limit_bytes=12 * 1024 * 1024),
+        )(*grads)
 
     return jax.shard_map(
         on_device,

time: 97.5 us -> 87.6 us (0.90)
  the two profiles are of different devices: /device:TPU:27 before, /device:TPU:0 now
where the time goes in v2:
time: 87.6 us; the launch traced here: 87.4 us
  Pallas kernels  86.8 us (99%)
    pallas_call x1, Pallas kernels, on_device(): pl.pallas_call(functools.partial(kernel, pipe_count, ctx_count), out_shap...  82.8 us
    pallas_call x1, Pallas kernels, on_device(): pl.pallas_call(place_kernel, out_shape=[jax.ShapeDtypeStruct(queries.shap...  4 us

profile of v2, /device:TPU:0, one launch (start us, length us, event | category | flops | bytes accessed | tf_op | source)
XLA Modules:
  0.0 87.4 jit_solution(14583248757519874145)
XLA Ops:
  0.6 82.8 %shard_map.94 = (bf16[16,384,256]{2,1,0:T(8,128)(2,1)S(1)}, bf16[16,384,256]{2,1,0:T(8,128)(2,1)S(1)}, bf16[16,384,256]{2,1,0:T(8,128)(2,1)S(1)}) custom-call(bf16[1,384,4096]{2,1,0:T(8,128)(2,1)} %q_hbm.1, bf16[1,384,4096]{2,1,0:T(8,128)(2,1)} %k_hbm.1, bf16[1,384,4096]{2,1,0:T(8,128)(2,1)} %v_hbm.1, bf16[1,384,4096]{2,1,0:T(8,128)(2,1)} %g_hbm.1, ...), custom_call_target="tpu_custom_call" | custom-call | tf_op jit(solution)/shard_map/pallas_call | solution.py:394
  83.4 4.0 %shard_map.95 = (bf16[1,384,4096]{2,1,0:T(8,128)(2,1)}, bf16[1,384,4096]{2,1,0:T(8,128)(2,1)}, bf16[1,384,4096]{2,1,0:T(8,128)(2,1)}) custom-call(bf16[16,384,256]{2,1,0:T(8,128)(2,1)S(1)} %get-tuple-element.6.in_q, bf16[16,384,256]{2,1,0:T(8,128)(2,1)S(1)} %get-tuple-element.7.in_k, bf16[16,384,256]{2,1,0:T(8,128)(2,1)S(1)} %get-tuple-element.8.in_v), custom_call_target="tpu_custom_call" | custom-call | tf_op jit(solution)/shard_map/pallas_call | solution.py:438

commit v3 on v2

--- a/solution.py
+++ b/solution.py
@@ -9,9 +9,10 @@
 
 MESH = pl.DeviceIdType.MESH
 LANES = 128
-CHUNK_HEADS = 2
+CHUNK_HEADS = 1
 IN_FLIGHT = 4
 SLOTS = 3
+PLACE_PARTS = 8
 MASKED = -1e30
 
 
@@ -36,8 +37,8 @@
     k_hbm,
     v_hbm,
     g_hbm,
-    decay_ref,
-    doc_ref,
+    decay_hbm,
+    doc_hbm,
     prefix_hbm,
     out_q,
     out_k,
@@ -56,15 +57,19 @@
     meta_all,
     link_s,
     cont_s,
+    decay_s,
+    doc_s,
+    total_s,
     state_s,
     odd_state_s,
     pair_s,
     pair_in_s,
-    odd_suffix_s,
+    suffix_s,
     suffix_in_s,
     inner_s,
     load_sem,
     prefix_sem,
+    small_sem,
     g_send,
     g_recv,
     meta_send,
@@ -151,7 +156,7 @@
 
     def suffix_copy(t):
         return pltpu.make_async_remote_copy(
-            src_ref=odd_suffix_s.at[t],
+            src_ref=suffix_s.at[t],
             dst_ref=suffix_in_s.at[t],
             send_sem=suffix_send.at[t],
             recv_sem=suffix_recv.at[t],
@@ -171,6 +176,10 @@
 
     for t in range(IN_FLIGHT):
         grad_copy(t).start()
+    decay_copy = pltpu.make_async_copy(decay_hbm.at[0], decay_s, small_sem.at[0])
+    doc_copy = pltpu.make_async_copy(doc_hbm, doc_s, small_sem.at[1])
+    decay_copy.start()
+    doc_copy.start()
 
     @pl.loop(0, chunks)
     def _(t):
@@ -183,11 +192,13 @@
     rows = lax.broadcasted_iota(jnp.int32, (length, length), 0)
     cols = lax.broadcasted_iota(jnp.int32, (length, length), 1)
     ordered = rows <= cols
+    decay_copy.wait()
+    doc_copy.wait()
     running = dot(
-        decay_ref[0], jnp.where(ordered, 1.0, 0.0), 1, 0, precision=lax.Precision.HIGHEST
+        decay_s[...], jnp.where(ordered, 1.0, 0.0), 1, 0, precision=lax.Precision.HIGHEST
     )
     run_s[...] = running
-    doc_row = doc_ref[...].astype(jnp.float32)
+    doc_row = doc_s[...].astype(jnp.float32)
     first_doc = jnp.broadcast_to(doc_row[:, 0:1], (8, LANES))
     last_doc = jnp.broadcast_to(doc_row[:, length - 1 : length], (8, LANES))
     meta_own[0:heads] = jnp.broadcast_to(
@@ -224,6 +235,9 @@
     head_mask_s[...] = jnp.where(doc_cols == first_doc[0:1], 1.0, 0.0) * cont_s[me][0:1]
     prefix_copy.wait()
 
+    def head_columns(h):
+        return pl.ds(pl.multiple_of(h * head_dim, head_dim), head_dim)
+
     def part(u):
         return slice(u * head_dim, (u + 1) * head_dim)
 
@@ -235,10 +249,11 @@
         load_copy(0, t).wait()
         for u in range(CHUNK_HEADS):
             weighted = head_weight(t * CHUNK_HEADS + u) * g_s[t, :, part(u)].astype(jnp.float32)
-            state_s[t, u] = dot(q_s[t, :, part(u)], weighted.astype(jnp.bfloat16), 0, 0)
+            total_s[u] = dot(q_s[t, :, part(u)], weighted.astype(jnp.bfloat16), 0, 0)
 
         @pl.when(odd == 1)
         def _():
+            state_s[t] = total_s[...].astype(jnp.bfloat16)
             state_copy(t).start()
 
         grad_copy(t).wait_send()
@@ -251,7 +266,8 @@
         state_copy(t).wait_recv()
         for u in range(CHUNK_HEADS):
             link = link_s[me, pl.ds(t * CHUNK_HEADS + u, 1), :]
-            pair_s[t, u] = state_s[t, u] + link * odd_state_s[t, u]
+            total = total_s[u] + link * odd_state_s[t, u].astype(jnp.float32)
+            pair_s[t, u] = total.astype(jnp.bfloat16)
         for d in range(1, reach + 1):
 
             @pl.when(pair >= d)
@@ -259,18 +275,19 @@
                 pair_copy(d, t).start()
 
     def stage_suffix(t):
-        odd_suffix_s[t] = jnp.zeros(odd_suffix_s.shape[1:], jnp.float32)
+        total_s[...] = jnp.zeros(total_s.shape, jnp.float32)
         for d in range(1, reach + 1):
 
             @pl.when(pair + d < pairs)
             def _():
                 pair_copy(d, t).wait_recv()
                 for u in range(CHUNK_HEADS):
-                    term = pair_in_s[d - 1, t, u]
+                    term = pair_in_s[d - 1, t, u].astype(jnp.float32)
                     for b in range(1, 2 * d - 1):
                         term = term * link_s[me + b, pl.ds(t * CHUNK_HEADS + u, 1), :]
-                    odd_suffix_s[t, u] += term
-
+                    total_s[u] += term
+
+        suffix_s[t] = total_s[...].astype(jnp.bfloat16)
         suffix_copy(t).start()
 
     def stage_inner(t, u):
@@ -295,7 +312,7 @@
                 grad_q[i] = piece if grad_q[i] is None else grad_q[i] + piece
         prefix = prefix_s[h].astype(jnp.bfloat16)
         grad_q = jnp.concatenate(grad_q, axis=0) + dot(g, prefix, 1, 1) * head_weight(h)
-        out_q[t, :, part(u)] = grad_q.astype(jnp.bfloat16)
+        out_q[:, head_columns(h)] = grad_q.astype(jnp.bfloat16)
 
     def stage_finish(t):
         slot = lax.rem(t, SLOTS)
@@ -305,16 +322,18 @@
             suffix_copy(t).wait_recv()
             for u in range(CHUNK_HEADS):
                 link = link_s[me + 1, pl.ds(t * CHUNK_HEADS + u, 1), :]
-                odd_suffix_s[t, u] = odd_state_s[t, u] + link * suffix_in_s[t, u]
+                carried = link * suffix_in_s[t, u].astype(jnp.float32)
+                total = odd_state_s[t, u].astype(jnp.float32) + carried
+                suffix_s[t, u] = total.astype(jnp.bfloat16)
 
         for u in range(CHUNK_HEADS):
             h = t * CHUNK_HEADS + u
-            suffix = odd_suffix_s[t, u].astype(jnp.bfloat16)
+            suffix = suffix_s[t, u]
             tail = jnp.exp(col_s[h, length - 1 : length, :] - col_s[h]) * tail_mask_s[...]
             grad_k = inner_s[slot, 0, :, part(u)] + dot(v_s[t, :, part(u)], suffix, 1, 1) * tail
             grad_v = inner_s[slot, 1, :, part(u)] + dot(k_s[t, :, part(u)], suffix, 1, 0) * tail
-            out_k[t, :, part(u)] = grad_k.astype(jnp.bfloat16)
-            out_v[t, :, part(u)] = grad_v.astype(jnp.bfloat16)
+            out_k[:, head_columns(h)] = grad_k.astype(jnp.bfloat16)
+            out_v[:, head_columns(h)] = grad_v.astype(jnp.bfloat16)
 
     @pl.loop(0, chunks + 2)
     def _(step):
@@ -323,16 +342,16 @@
             stage_state(step)
             load_copy(1, step).wait()
             load_copy(2, step).wait()
-            for u in range(CHUNK_HEADS - 1):
+            stage_inner(step, 0)
+
+        @pl.when((step < chunks) & (odd == 0))
+        def _():
+            stage_pair(step)
+
+        @pl.when(step < chunks)
+        def _():
+            for u in range(1, CHUNK_HEADS):
                 stage_inner(step, u)
-
-        @pl.when((step < chunks) & (odd == 0))
-        def _():
-            stage_pair(step)
-
-        @pl.when(step < chunks)
-        def _():
-            stage_inner(step, CHUNK_HEADS - 1)
 
         @pl.when((step >= 1) & (step < chunks + 1) & (odd == 1))
         def _():
@@ -360,14 +379,14 @@
 
 
 def place_kernel(in_q, in_k, in_v, out_q, out_k, out_v, sem):
-    chunks, _, chunk_cols = in_q.shape
-    copies = [
-        pltpu.make_async_copy(
-            source.at[t], target.at[0, :, t * chunk_cols : (t + 1) * chunk_cols], sem.at[i, t]
-        )
-        for i, (source, target) in enumerate(((in_q, out_q), (in_k, out_k), (in_v, out_v)))
-        for t in range(chunks)
-    ]
+    rows = in_q.shape[0] // PLACE_PARTS
+    copies = []
+    for j in range(PLACE_PARTS):
+        span = slice(j * rows, (j + 1) * rows)
+        for i, (source, target) in enumerate(((in_q, out_q), (in_k, out_k), (in_v, out_v))):
+            copies.append(
+                pltpu.make_async_copy(source.at[span], target.at[0, span], sem.at[i, j])
+            )
     for copy in copies:
         copy.start()
     for copy in copies:
@@ -388,13 +407,13 @@
         vmem_spec = pl.BlockSpec(memory_space=pltpu.VMEM)
         f32, bf16 = jnp.float32, jnp.bfloat16
         rows = pltpu.VMEM((chunks, length, chunk_cols), bf16)
-        states = pltpu.VMEM((chunks, CHUNK_HEADS, head_dim, head_dim), f32)
+        states = pltpu.VMEM((chunks, CHUNK_HEADS, head_dim, head_dim), bf16)
         mask = pltpu.VMEM((length, LANES), f32)
         dma = pltpu.SemaphoreType.DMA
         grads = pl.pallas_call(
             functools.partial(kernel, pipe_count, ctx_count),
-            out_shape=[pltpu.VMEM((chunks, length, chunk_cols), bf16)] * 3,
-            in_specs=[any_spec] * 4 + [vmem_spec] * 2 + [any_spec],
+            out_shape=[pltpu.VMEM((length, width), bf16)] * 3,
+            in_specs=[any_spec] * 7,
             out_specs=[vmem_spec] * 3,
             scratch_shapes=[
                 rows,
@@ -411,15 +430,19 @@
                 pltpu.VMEM((ctx_count, heads + 16, LANES), f32),
                 pltpu.VMEM((ctx_count, heads, LANES), f32),
                 pltpu.VMEM((ctx_count, 8, LANES), f32),
+                pltpu.VMEM((heads, length), f32),
+                pltpu.VMEM((1, length), jnp.int32),
+                pltpu.VMEM((CHUNK_HEADS, head_dim, head_dim), f32),
                 states,
                 states,
                 states,
-                pltpu.VMEM((reach, chunks, CHUNK_HEADS, head_dim, head_dim), f32),
+                pltpu.VMEM((reach, chunks, CHUNK_HEADS, head_dim, head_dim), bf16),
                 states,
                 states,
                 pltpu.VMEM((SLOTS, 2, length, chunk_cols), f32),
                 dma((3, chunks)),
                 dma,
+                dma((2,)),
                 dma((chunks,)),
                 dma((chunks,)),
                 dma((ctx_count,)),
@@ -432,7 +455,7 @@
                 dma((chunks,)),
             ],
             compiler_params=pltpu.CompilerParams(
-                collective_id=0, has_side_effects=True, vmem_limit_bytes=50 * 1024 * 1024
+                collective_id=0, has_side_effects=True, vmem_limit_bytes=46 * 1024 * 1024
             ),
         )(queries, key_rows, value_rows, next_grads, log_decay, doc_ids, prefix_states)
         return pl.pallas_call(
@@ -440,7 +463,7 @@
             out_shape=[jax.ShapeDtypeStruct(queries.shape, bf16)] * 3,
             in_specs=[vmem_spec] * 3,
             out_specs=[any_spec] * 3,
-            scratch_shapes=[dma((3, chunks))],
+            scratch_shapes=[dma((3, PLACE_PARTS))],
             compiler_params=pltpu.CompilerParams(vmem_limit_bytes=12 * 1024 * 1024),
         )(*grads)
 

time: 87.6 us -> 88.6 us (1.011)
  Pallas kernels: 86.8 us -> 87.8 us
    pallas_call x1, Pallas kernels: 82.8 us -> 84 us  [on_device(): pl.pallas_call(functools.partial(kernel, pipe_count, ctx_count), out_shap...]
where the time goes in v3:
time: 88.6 us; the launch traced here: 88.5 us
  Pallas kernels  87.8 us (99%)
    pallas_call x1, Pallas kernels, on_device(): pl.pallas_call(functools.partial(kernel, pipe_count, ctx_count), out_shap...  84 us
    pallas_call x1, Pallas kernels, on_device(): pl.pallas_call(place_kernel, out_shape=[jax.ShapeDtypeStruct(queries.shap...  3.8 us

profile of v3, /device:TPU:0, one launch (start us, length us, event | category | flops | bytes accessed | tf_op | source)
XLA Modules:
  0.0 88.5 jit_solution(9517837302557097723)
XLA Ops:
  0.6 84.0 %shard_map.94 = (bf16[384,4096]{1,0:T(8,128)(2,1)S(1)}, bf16[384,4096]{1,0:T(8,128)(2,1)S(1)}, bf16[384,4096]{1,0:T(8,128)(2,1)S(1)}) custom-call(bf16[1,384,4096]{2,1,0:T(8,128)(2,1)} %q_hbm.1, bf16[1,384,4096]{2,1,0:T(8,128)(2,1)} %k_hbm.1, bf16[1,384,4096]{2,1,0:T(8,128)(2,1)} %v_hbm.1, bf16[1,384,4096]{2,1,0:T(8,128)(2,1)} %g_hbm.1, ...), custom_call_target="tpu_custom_call" | custom-call | tf_op jit(solution)/shard_map/pallas_call | solution.py:413
  84.7 3.8 %shard_map.95 = (bf16[1,384,4096]{2,1,0:T(8,128)(2,1)}, bf16[1,384,4096]{2,1,0:T(8,128)(2,1)}, bf16[1,384,4096]{2,1,0:T(8,128)(2,1)}) custom-call(bf16[384,4096]{1,0:T(8,128)(2,1)S(1)} %get-tuple-element.6.in_q, bf16[384,4096]{1,0:T(8,128)(2,1)S(1)} %get-tuple-element.7.in_k, bf16[384,4096]{1,0:T(8,128)(2,1)S(1)} %get-tuple-element.8.in_v), custom_call_target="tpu_custom_call" | custom-call | tf_op jit(solution)/shard_map/pallas_call | solution.py:461

commit v4 on v3

--- a/solution.py
+++ b/solution.py
@@ -11,7 +11,10 @@
 LANES = 128
 CHUNK_HEADS = 1
 IN_FLIGHT = 4
-SLOTS = 3
+PAIR_LAG = 1
+SUFFIX_LAG = 3
+FINISH_LAG = 5
+SLOTS = FINISH_LAG + 1
 PLACE_PARTS = 8
 MASKED = -1e30
 
@@ -60,6 +63,7 @@
     decay_s,
     doc_s,
     total_s,
+    sum_s,
     state_s,
     odd_state_s,
     pair_s,
@@ -249,11 +253,11 @@
         load_copy(0, t).wait()
         for u in range(CHUNK_HEADS):
             weighted = head_weight(t * CHUNK_HEADS + u) * g_s[t, :, part(u)].astype(jnp.float32)
-            total_s[u] = dot(q_s[t, :, part(u)], weighted.astype(jnp.bfloat16), 0, 0)
+            total_s[lax.rem(t, 2), u] = dot(q_s[t, :, part(u)], weighted.astype(jnp.bfloat16), 0, 0)
 
         @pl.when(odd == 1)
         def _():
-            state_s[t] = total_s[...].astype(jnp.bfloat16)
+            state_s[t] = total_s[lax.rem(t, 2)].astype(jnp.bfloat16)
             state_copy(t).start()
 
         grad_copy(t).wait_send()
@@ -266,7 +270,7 @@
         state_copy(t).wait_recv()
         for u in range(CHUNK_HEADS):
             link = link_s[me, pl.ds(t * CHUNK_HEADS + u, 1), :]
-            total = total_s[u] + link * odd_state_s[t, u].astype(jnp.float32)
+            total = total_s[lax.rem(t, 2), u] + link * odd_state_s[t, u].astype(jnp.float32)
             pair_s[t, u] = total.astype(jnp.bfloat16)
         for d in range(1, reach + 1):
 
@@ -275,7 +279,7 @@
                 pair_copy(d, t).start()
 
     def stage_suffix(t):
-        total_s[...] = jnp.zeros(total_s.shape, jnp.float32)
+        sum_s[...] = jnp.zeros(sum_s.shape, jnp.float32)
         for d in range(1, reach + 1):
 
             @pl.when(pair + d < pairs)
@@ -285,9 +289,9 @@
                     term = pair_in_s[d - 1, t, u].astype(jnp.float32)
                     for b in range(1, 2 * d - 1):
                         term = term * link_s[me + b, pl.ds(t * CHUNK_HEADS + u, 1), :]
-                    total_s[u] += term
-
-        suffix_s[t] = total_s[...].astype(jnp.bfloat16)
+                    sum_s[u] += term
+
+        suffix_s[t] = sum_s[...].astype(jnp.bfloat16)
         suffix_copy(t).start()
 
     def stage_inner(t, u):
@@ -335,31 +339,27 @@
             out_k[:, head_columns(h)] = grad_k.astype(jnp.bfloat16)
             out_v[:, head_columns(h)] = grad_v.astype(jnp.bfloat16)
 
-    @pl.loop(0, chunks + 2)
+    @pl.loop(0, chunks + FINISH_LAG)
     def _(step):
+        @pl.when((step >= PAIR_LAG) & (step < chunks + PAIR_LAG) & (odd == 0))
+        def _():
+            stage_pair(step - PAIR_LAG)
+
+        @pl.when((step >= SUFFIX_LAG) & (step < chunks + SUFFIX_LAG) & (odd == 1))
+        def _():
+            stage_suffix(step - SUFFIX_LAG)
+
         @pl.when(step < chunks)
         def _():
             stage_state(step)
             load_copy(1, step).wait()
             load_copy(2, step).wait()
-            stage_inner(step, 0)
-
-        @pl.when((step < chunks) & (odd == 0))
-        def _():
-            stage_pair(step)
-
-        @pl.when(step < chunks)
-        def _():
-            for u in range(1, CHUNK_HEADS):
+            for u in range(CHUNK_HEADS):
                 stage_inner(step, u)
 
-        @pl.when((step >= 1) & (step < chunks + 1) & (odd == 1))
-        def _():
-            stage_suffix(step - 1)
-
-        @pl.when(step >= 2)
-        def _():
-            stage_finish(step - 2)
+        @pl.when(step >= FINISH_LAG)
+        def _():
+            stage_finish(step - FINISH_LAG)
 
     for k in range(1, ctx_count):
         meta_copy(k).wait_send()
@@ -432,6 +432,7 @@
                 pltpu.VMEM((ctx_count, 8, LANES), f32),
                 pltpu.VMEM((heads, length), f32),
                 pltpu.VMEM((1, length), jnp.int32),
+                pltpu.VMEM((2, CHUNK_HEADS, head_dim, head_dim), f32),
                 pltpu.VMEM((CHUNK_HEADS, head_dim, head_dim), f32),
                 states,
                 states,

time: 88.6 us -> 87.6 us (0.989)
  Pallas kernels: 87.8 us -> 86.8 us
    pallas_call x1, Pallas kernels: 84 us -> 83 us  [on_device(): pl.pallas_call(functools.partial(kernel, pipe_count, ctx_count), out_shap...]
where the time goes in v4:
time: 87.6 us; the launch traced here: 87.5 us
  Pallas kernels  86.8 us (99%)
    pallas_call x1, Pallas kernels, on_device(): pl.pallas_call(functools.partial(kernel, pipe_count, ctx_count), out_shap...  83 us
    pallas_call x1, Pallas kernels, on_device(): pl.pallas_call(place_kernel, out_shape=[jax.ShapeDtypeStruct(queries.shap...  3.8 us

profile of v4, /device:TPU:0, one launch (start us, length us, event | category | flops | bytes accessed | tf_op | source)
XLA Modules:
  0.0 87.5 jit_solution(8997885880266887369)
XLA Ops:
  0.6 83.0 %shard_map.94 = (bf16[384,4096]{1,0:T(8,128)(2,1)S(1)}, bf16[384,4096]{1,0:T(8,128)(2,1)S(1)}, bf16[384,4096]{1,0:T(8,128)(2,1)S(1)}) custom-call(bf16[1,384,4096]{2,1,0:T(8,128)(2,1)} %q_hbm.1, bf16[1,384,4096]{2,1,0:T(8,128)(2,1)} %k_hbm.1, bf16[1,384,4096]{2,1,0:T(8,128)(2,1)} %v_hbm.1, bf16[1,384,4096]{2,1,0:T(8,128)(2,1)} %g_hbm.1, ...), custom_call_target="tpu_custom_call" | custom-call | tf_op jit(solution)/shard_map/pallas_call | solution.py:413
  83.7 3.8 %shard_map.95 = (bf16[1,384,4096]{2,1,0:T(8,128)(2,1)}, bf16[1,384,4096]{2,1,0:T(8,128)(2,1)}, bf16[1,384,4096]{2,1,0:T(8,128)(2,1)}) custom-call(bf16[384,4096]{1,0:T(8,128)(2,1)S(1)} %get-tuple-element.6.in_q, bf16[384,4096]{1,0:T(8,128)(2,1)S(1)} %get-tuple-element.7.in_k, bf16[384,4096]{1,0:T(8,128)(2,1)S(1)} %get-tuple-element.8.in_v), custom_call_target="tpu_custom_call" | custom-call | tf_op jit(solution)/shard_map/pallas_call | solution.py:462

commit v5 on v4

--- a/solution.py
+++ b/solution.py
@@ -13,7 +13,7 @@
 IN_FLIGHT = 4
 PAIR_LAG = 1
 SUFFIX_LAG = 3
-FINISH_LAG = 5
+FINISH_LAG = 4
 SLOTS = FINISH_LAG + 1
 PLACE_PARTS = 8
 MASKED = -1e30
@@ -50,6 +50,7 @@
     k_s,
     v_s,
     g_s,
+    g_own_s,
     prefix_s,
     run_s,
     col_s,
@@ -98,6 +99,86 @@
     earlier = lax.rem(section + pipe_count - 1, pipe_count)
     later = lax.rem(section + 1, pipe_count)
 
+    def columns(t):
+        return pl.ds(pl.multiple_of(t * chunk_cols, chunk_cols), chunk_cols)
+
+    def grad_copy(t):
+        return pltpu.make_async_remote_copy(
+            src_ref=g_own_s.at[t],
+            dst_ref=g_s.at[t],
+            send_sem=g_send.at[t],
+            recv_sem=g_recv.at[t],
+            device_id={"pipe": earlier},
+            device_id_type=MESH,
+        )
+
+    def load_copy(i, t):
+        source, target = ((q_hbm, q_s), (k_hbm, k_s), (v_hbm, v_s), (g_hbm, g_own_s))[i]
+        return pltpu.make_async_copy(
+            source.at[0, :, columns(t)], target.at[t], load_sem.at[i, t]
+        )
+
+    def meta_copy(k):
+        return pltpu.make_async_remote_copy(
+            src_ref=meta_own,
+            dst_ref=meta_all.at[me],
+            send_sem=meta_send.at[k],
+            recv_sem=meta_recv.at[k],
+            device_id={"ctx": lax.rem(me + k, ctx_count)},
+            device_id_type=MESH,
+        )
+
+    def meta_arrival(k):
+        return pltpu.make_async_remote_copy(
+            src_ref=meta_own,
+            dst_ref=meta_all.at[lax.rem(me + ctx_count - k, ctx_count)],
+            send_sem=meta_send.at[k],
+            recv_sem=meta_recv.at[k],
+            device_id={"ctx": lax.rem(me + k, ctx_count)},
+            device_id_type=MESH,
+        )
+
+    partner = me + 1 - 2 * odd
+
+    def state_copy(t):
+        return pltpu.make_async_remote_copy(
+            src_ref=state_s.at[t],
+            dst_ref=odd_state_s.at[t],
+            send_sem=state_send.at[t],
+            recv_sem=state_recv.at[t],
+            device_id={"ctx": partner},
+            device_id_type=MESH,
+        )
+
+    def suffix_copy(t):
+        return pltpu.make_async_remote_copy(
+            src_ref=suffix_s.at[t],
+            dst_ref=suffix_in_s.at[t],
+            send_sem=suffix_send.at[t],
+            recv_sem=suffix_recv.at[t],
+            device_id={"ctx": partner},
+            device_id_type=MESH,
+        )
+
+    def pair_copy(d, t):
+        return pltpu.make_async_remote_copy(
+            src_ref=pair_s.at[t],
+            dst_ref=pair_in_s.at[d - 1, t],
+            send_sem=pair_send.at[d - 1, t],
+            recv_sem=pair_recv.at[d - 1, t],
+            device_id={"ctx": lax.rem(me - 2 * d + 1 + ctx_count, ctx_count)},
+            device_id_type=MESH,
+        )
+
+    @pl.loop(0, chunks)
+    def _(t):
+        load_copy(3, t).start()
+
+    decay_copy = pltpu.make_async_copy(decay_hbm.at[0], decay_s, small_sem.at[0])
+    doc_copy = pltpu.make_async_copy(doc_hbm, doc_s, small_sem.at[1])
+    decay_copy.start()
+    doc_copy.start()
+
     barrier = pltpu.get_barrier_semaphore()
     pl.semaphore_signal(barrier, inc=1, device_id={"pipe": earlier}, device_id_type=MESH)
     pl.semaphore_signal(barrier, inc=1, device_id={"pipe": later}, device_id_type=MESH)
@@ -107,83 +188,9 @@
         )
     pl.semaphore_wait(barrier, ctx_count + 1)
 
-    def columns(t):
-        return pl.ds(pl.multiple_of(t * chunk_cols, chunk_cols), chunk_cols)
-
-    def grad_copy(t):
-        return pltpu.make_async_remote_copy(
-            src_ref=g_hbm.at[0, :, columns(t)],
-            dst_ref=g_s.at[t],
-            send_sem=g_send.at[t],
-            recv_sem=g_recv.at[t],
-            device_id={"pipe": earlier},
-            device_id_type=MESH,
-        )
-
-    def load_copy(i, t):
-        source, target = ((q_hbm, q_s), (k_hbm, k_s), (v_hbm, v_s))[i]
-        return pltpu.make_async_copy(
-            source.at[0, :, columns(t)], target.at[t], load_sem.at[i, t]
-        )
-
-    def meta_copy(k):
-        return pltpu.make_async_remote_copy(
-            src_ref=meta_own,
-            dst_ref=meta_all.at[me],
-            send_sem=meta_send.at[k],
-            recv_sem=meta_recv.at[k],
-            device_id={"ctx": lax.rem(me + k, ctx_count)},
-            device_id_type=MESH,
-        )
-
-    def meta_arrival(k):
-        return pltpu.make_async_remote_copy(
-            src_ref=meta_own,
-            dst_ref=meta_all.at[lax.rem(me + ctx_count - k, ctx_count)],
-            send_sem=meta_send.at[k],
-            recv_sem=meta_recv.at[k],
-            device_id={"ctx": lax.rem(me + k, ctx_count)},
-            device_id_type=MESH,
-        )
-
-    partner = me + 1 - 2 * odd
-
-    def state_copy(t):
-        return pltpu.make_async_remote_copy(
-            src_ref=state_s.at[t],
-            dst_ref=odd_state_s.at[t],
-            send_sem=state_send.at[t],
-            recv_sem=state_recv.at[t],
-            device_id={"ctx": partner},
-            device_id_type=MESH,
-        )
-
-    def suffix_copy(t):
-        return pltpu.make_async_remote_copy(
-            src_ref=suffix_s.at[t],
-            dst_ref=suffix_in_s.at[t],
-            send_sem=suffix_send.at[t],
-            recv_sem=suffix_recv.at[t],
-            device_id={"ctx": partner},
-            device_id_type=MESH,
-        )
-
-    def pair_copy(d, t):
-        return pltpu.make_async_remote_copy(
-            src_ref=pair_s.at[t],
-            dst_ref=pair_in_s.at[d - 1, t],
-            send_sem=pair_send.at[d - 1, t],
-            recv_sem=pair_recv.at[d - 1, t],
-            device_id={"ctx": lax.rem(me - 2 * d + 1 + ctx_count, ctx_count)},
-            device_id_type=MESH,
-        )
-
     for t in range(IN_FLIGHT):
+        load_copy(3, t).wait()
         grad_copy(t).start()
-    decay_copy = pltpu.make_async_copy(decay_hbm.at[0], decay_s, small_sem.at[0])
-    doc_copy = pltpu.make_async_copy(doc_hbm, doc_s, small_sem.at[1])
-    decay_copy.start()
-    doc_copy.start()
 
     @pl.loop(0, chunks)
     def _(t):
@@ -250,6 +257,13 @@
 
     def stage_state(t):
         grad_copy(t).wait_recv()
+        grad_copy(t).wait_send()
+
+        @pl.when(t + IN_FLIGHT < chunks)
+        def _():
+            load_copy(3, t + IN_FLIGHT).wait()
+            grad_copy(t + IN_FLIGHT).start()
+
         load_copy(0, t).wait()
         for u in range(CHUNK_HEADS):
             weighted = head_weight(t * CHUNK_HEADS + u) * g_s[t, :, part(u)].astype(jnp.float32)
@@ -260,11 +274,6 @@
             state_s[t] = total_s[lax.rem(t, 2)].astype(jnp.bfloat16)
             state_copy(t).start()
 
-        grad_copy(t).wait_send()
-
-        @pl.when(t + IN_FLIGHT < chunks)
-        def _():
-            grad_copy(t + IN_FLIGHT).start()
 
     def stage_pair(t):
         state_copy(t).wait_recv()
@@ -416,6 +425,7 @@
             in_specs=[any_spec] * 7,
             out_specs=[vmem_spec] * 3,
             scratch_shapes=[
+                rows,
                 rows,
                 rows,
                 rows,
@@ -441,7 +451,7 @@
                 states,
                 states,
                 pltpu.VMEM((SLOTS, 2, length, chunk_cols), f32),
-                dma((3, chunks)),
+                dma((4, chunks)),
                 dma,
                 dma((2,)),
                 dma((chunks,)),

time: 87.6 us -> 88 us (level)
  no operation moved by 1% of the time
where the time goes in v5:
time: 88 us; the launch traced here: 87.9 us
  Pallas kernels  87.2 us (99%)
    pallas_call x1, Pallas kernels, on_device(): pl.pallas_call(functools.partial(kernel, pipe_count, ctx_count), out_shap...  83.4 us
    pallas_call x1, Pallas kernels, on_device(): pl.pallas_call(place_kernel, out_shape=[jax.ShapeDtypeStruct(queries.shap...  3.8 us

profile of v5, /device:TPU:0, one launch (start us, length us, event | category | flops | bytes accessed | tf_op | source)
XLA Modules:
  0.0 87.9 jit_solution(13344664193436751043)
XLA Ops:
  0.6 83.4 %shard_map.94 = (bf16[384,4096]{1,0:T(8,128)(2,1)S(1)}, bf16[384,4096]{1,0:T(8,128)(2,1)S(1)}, bf16[384,4096]{1,0:T(8,128)(2,1)S(1)}) custom-call(bf16[1,384,4096]{2,1,0:T(8,128)(2,1)} %q_hbm.1, bf16[1,384,4096]{2,1,0:T(8,128)(2,1)} %k_hbm.1, bf16[1,384,4096]{2,1,0:T(8,128)(2,1)} %v_hbm.1, bf16[1,384,4096]{2,1,0:T(8,128)(2,1)} %g_hbm.1, ...), custom_call_target="tpu_custom_call" | custom-call | tf_op jit(solution)/shard_map/pallas_call | solution.py:422
  84.1 3.8 %shard_map.95 = (bf16[1,384,4096]{2,1,0:T(8,128)(2,1)}, bf16[1,384,4096]{2,1,0:T(8,128)(2,1)}, bf16[1,384,4096]{2,1,0:T(8,128)(2,1)}) custom-call(bf16[384,4096]{1,0:T(8,128)(2,1)S(1)} %get-tuple-element.6.in_q, bf16[384,4096]{1,0:T(8,128)(2,1)S(1)} %get-tuple-element.7.in_k, bf16[384,4096]{1,0:T(8,128)(2,1)S(1)} %get-tuple-element.8.in_v), custom_call_target="tpu_custom_call" | custom-call | tf_op jit(solution)/shard_map/pallas_call | solution.py:472

commit v6 on v4

--- a/solution.py
+++ b/solution.py
@@ -11,9 +11,8 @@
 LANES = 128
 CHUNK_HEADS = 1
 IN_FLIGHT = 4
-PAIR_LAG = 1
 SUFFIX_LAG = 3
-FINISH_LAG = 5
+FINISH_LAG = 4
 SLOTS = FINISH_LAG + 1
 PLACE_PARTS = 8
 MASKED = -1e30
@@ -62,12 +61,10 @@
     cont_s,
     decay_s,
     doc_s,
-    total_s,
     sum_s,
     state_s,
     odd_state_s,
-    pair_s,
-    pair_in_s,
+    later_in_s,
     suffix_s,
     suffix_in_s,
     inner_s,
@@ -80,8 +77,8 @@
     meta_recv,
     state_send,
     state_recv,
-    pair_send,
-    pair_recv,
+    later_send,
+    later_recv,
     suffix_send,
     suffix_recv,
 ):
@@ -168,13 +165,13 @@
             device_id_type=MESH,
         )
 
-    def pair_copy(d, t):
-        return pltpu.make_async_remote_copy(
-            src_ref=pair_s.at[t],
-            dst_ref=pair_in_s.at[d - 1, t],
-            send_sem=pair_send.at[d - 1, t],
-            recv_sem=pair_recv.at[d - 1, t],
-            device_id={"ctx": lax.rem(me - 2 * d + 1 + ctx_count, ctx_count)},
+    def later_copy(d, sender, t):
+        return pltpu.make_async_remote_copy(
+            src_ref=state_s.at[t],
+            dst_ref=later_in_s.at[d - 1, sender, t],
+            send_sem=later_send.at[d - 1, t],
+            recv_sem=later_recv.at[d - 1, sender, t],
+            device_id={"ctx": lax.rem(me - odd - 2 * d + 1 + ctx_count, ctx_count)},
             device_id_type=MESH,
         )
 
@@ -253,30 +250,23 @@
         load_copy(0, t).wait()
         for u in range(CHUNK_HEADS):
             weighted = head_weight(t * CHUNK_HEADS + u) * g_s[t, :, part(u)].astype(jnp.float32)
-            total_s[lax.rem(t, 2), u] = dot(q_s[t, :, part(u)], weighted.astype(jnp.bfloat16), 0, 0)
-
-        @pl.when(odd == 1)
-        def _():
-            state_s[t] = total_s[lax.rem(t, 2)].astype(jnp.bfloat16)
-            state_copy(t).start()
-
-        grad_copy(t).wait_send()
-
-        @pl.when(t + IN_FLIGHT < chunks)
-        def _():
-            grad_copy(t + IN_FLIGHT).start()
-
-    def stage_pair(t):
-        state_copy(t).wait_recv()
-        for u in range(CHUNK_HEADS):
-            link = link_s[me, pl.ds(t * CHUNK_HEADS + u, 1), :]
-            total = total_s[lax.rem(t, 2), u] + link * odd_state_s[t, u].astype(jnp.float32)
-            pair_s[t, u] = total.astype(jnp.bfloat16)
+            state = dot(q_s[t, :, part(u)], weighted.astype(jnp.bfloat16), 0, 0)
+            state_s[t, u] = state.astype(jnp.bfloat16)
         for d in range(1, reach + 1):
 
             @pl.when(pair >= d)
             def _():
-                pair_copy(d, t).start()
+                later_copy(d, odd, t).start()
+
+        @pl.when(odd == 1)
+        def _():
+            state_copy(t).start()
+
+        grad_copy(t).wait_send()
+
+        @pl.when(t + IN_FLIGHT < chunks)
+        def _():
+            grad_copy(t + IN_FLIGHT).start()
 
     def stage_suffix(t):
         sum_s[...] = jnp.zeros(sum_s.shape, jnp.float32)
@@ -284,12 +274,13 @@
 
             @pl.when(pair + d < pairs)
             def _():
-                pair_copy(d, t).wait_recv()
-                for u in range(CHUNK_HEADS):
-                    term = pair_in_s[d - 1, t, u].astype(jnp.float32)
-                    for b in range(1, 2 * d - 1):
-                        term = term * link_s[me + b, pl.ds(t * CHUNK_HEADS + u, 1), :]
-                    sum_s[u] += term
+                for sender in range(2):
+                    later_copy(d, sender, t).wait_recv()
+                    for u in range(CHUNK_HEADS):
+                        term = later_in_s[d - 1, sender, t, u].astype(jnp.float32)
+                        for b in range(1, 2 * d - 1 + sender):
+                            term = term * link_s[me + b, pl.ds(t * CHUNK_HEADS + u, 1), :]
+                        sum_s[u] += term
 
         suffix_s[t] = sum_s[...].astype(jnp.bfloat16)
         suffix_copy(t).start()
@@ -323,6 +314,7 @@
 
         @pl.when(odd == 0)
         def _():
+            state_copy(t).wait_recv()
             suffix_copy(t).wait_recv()
             for u in range(CHUNK_HEADS):
                 link = link_s[me + 1, pl.ds(t * CHUNK_HEADS + u, 1), :]
@@ -341,10 +333,6 @@
 
     @pl.loop(0, chunks + FINISH_LAG)
     def _(step):
-        @pl.when((step >= PAIR_LAG) & (step < chunks + PAIR_LAG) & (odd == 0))
-        def _():
-            stage_pair(step - PAIR_LAG)
-
         @pl.when((step >= SUFFIX_LAG) & (step < chunks + SUFFIX_LAG) & (odd == 1))
         def _():
             stage_suffix(step - SUFFIX_LAG)
@@ -373,9 +361,9 @@
 
         for d in range(1, reach + 1):
 
-            @pl.when((odd == 0) & (pair >= d))
+            @pl.when(pair >= d)
             def _():
-                pair_copy(d, t).wait_send()
+                later_copy(d, odd, t).wait_send()
 
 
 def place_kernel(in_q, in_k, in_v, out_q, out_k, out_v, sem):
@@ -432,12 +420,10 @@
                 pltpu.VMEM((ctx_count, 8, LANES), f32),
                 pltpu.VMEM((heads, length), f32),
                 pltpu.VMEM((1, length), jnp.int32),
-                pltpu.VMEM((2, CHUNK_HEADS, head_dim, head_dim), f32),
                 pltpu.VMEM((CHUNK_HEADS, head_dim, head_dim), f32),
                 states,
                 states,
-                states,
-                pltpu.VMEM((reach, chunks, CHUNK_HEADS, head_dim, head_dim), bf16),
+                pltpu.VMEM((reach, 2, chunks, CHUNK_HEADS, head_dim, head_dim), bf16),
                 states,
                 states,
                 pltpu.VMEM((SLOTS, 2, length, chunk_cols), f32),
@@ -451,7 +437,7 @@
                 dma((chunks,)),
                 dma((chunks,)),
                 dma((reach, chunks)),
-                dma((reach, chunks)),
+                dma((reach, 2, chunks)),
                 dma((chunks,)),
                 dma((chunks,)),
             ],

time: 87.6 us -> 87.1 us (level)
  no operation moved by 1% of the time
where the time goes in v6:
time: 87.1 us; the launch traced here: 86.9 us
  Pallas kernels  86.3 us (99%)
    pallas_call x1, Pallas kernels, on_device(): pl.pallas_call(functools.partial(kernel, pipe_count, ctx_count), out_shap...  82.5 us
    pallas_call x1, Pallas kernels, on_device(): pl.pallas_call(place_kernel, out_shape=[jax.ShapeDtypeStruct(queries.shap...  3.8 us

profile of v6, /device:TPU:0, one launch (start us, length us, event | category | flops | bytes accessed | tf_op | source)
XLA Modules:
  0.0 86.9 jit_solution(11159241578272224071)
XLA Ops:
  0.6 82.5 %shard_map.94 = (bf16[384,4096]{1,0:T(8,128)(2,1)S(1)}, bf16[384,4096]{1,0:T(8,128)(2,1)S(1)}, bf16[384,4096]{1,0:T(8,128)(2,1)S(1)}) custom-call(bf16[1,384,4096]{2,1,0:T(8,128)(2,1)} %q_hbm.1, bf16[1,384,4096]{2,1,0:T(8,128)(2,1)} %k_hbm.1, bf16[1,384,4096]{2,1,0:T(8,128)(2,1)} %v_hbm.1, bf16[1,384,4096]{2,1,0:T(8,128)(2,1)} %g_hbm.1, ...), custom_call_target="tpu_custom_call" | custom-call | tf_op jit(solution)/shard_map/pallas_call | solution.py:401
  83.1 3.8 %shard_map.95 = (bf16[1,384,4096]{2,1,0:T(8,128)(2,1)}, bf16[1,384,4096]{2,1,0:T(8,128)(2,1)}, bf16[1,384,4096]{2,1,0:T(8,128)(2,1)}) custom-call(bf16[384,4096]{1,0:T(8,128)(2,1)S(1)} %get-tuple-element.6.in_q, bf16[384,4096]{1,0:T(8,128)(2,1)S(1)} %get-tuple-element.7.in_k, bf16[384,4096]{1,0:T(8,128)(2,1)S(1)} %get-tuple-element.8.in_v), custom_call_target="tpu_custom_call" | custom-call | tf_op jit(solution)/shard_map/pallas_call | solution.py:448

commit v7 on v6

--- a/solution.py
+++ b/solution.py
@@ -10,7 +10,7 @@
 MESH = pl.DeviceIdType.MESH
 LANES = 128
 CHUNK_HEADS = 1
-IN_FLIGHT = 4
+IN_FLIGHT = 3
 SUFFIX_LAG = 3
 FINISH_LAG = 4
 SLOTS = FINISH_LAG + 1
@@ -375,8 +375,8 @@
             copies.append(
                 pltpu.make_async_copy(source.at[span], target.at[0, span], sem.at[i, j])
             )
-    for copy in copies:
-        copy.start()
+    for n, copy in enumerate(copies):
+        copy.start(priority=n % 2)
     for copy in copies:
         copy.wait()
 

time: 87.1 us -> 87.1 us (level)
  no operation moved by 1% of the time
where the time goes in v7:
time: 87.1 us; the launch traced here: 86.9 us
  Pallas kernels  86.3 us (99%)
    pallas_call x1, Pallas kernels, on_device(): pl.pallas_call(functools.partial(kernel, pipe_count, ctx_count), out_shap...  82.5 us
    pallas_call x1, Pallas kernels, on_device(): pl.pallas_call(place_kernel, out_shape=[jax.ShapeDtypeStruct(queries.shap...  3.8 us

profile of v7, /device:TPU:0, one launch (start us, length us, event | category | flops | bytes accessed | tf_op | source)
XLA Modules:
  0.0 86.9 jit_solution(7751911635020891553)
XLA Ops:
  0.6 82.5 %shard_map.94 = (bf16[384,4096]{1,0:T(8,128)(2,1)S(1)}, bf16[384,4096]{1,0:T(8,128)(2,1)S(1)}, bf16[384,4096]{1,0:T(8,128)(2,1)S(1)}) custom-call(bf16[1,384,4096]{2,1,0:T(8,128)(2,1)} %q_hbm.1, bf16[1,384,4096]{2,1,0:T(8,128)(2,1)} %k_hbm.1, bf16[1,384,4096]{2,1,0:T(8,128)(2,1)} %v_hbm.1, bf16[1,384,4096]{2,1,0:T(8,128)(2,1)} %g_hbm.1, ...), custom_call_target="tpu_custom_call" | custom-call | tf_op jit(solution)/shard_map/pallas_call | solution.py:401
  83.1 3.8 %shard_map.95 = (bf16[1,384,4096]{2,1,0:T(8,128)(2,1)}, bf16[1,384,4096]{2,1,0:T(8,128)(2,1)}, bf16[1,384,4096]{2,1,0:T(8,128)(2,1)}) custom-call(bf16[384,4096]{1,0:T(8,128)(2,1)S(1)} %get-tuple-element.6.in_q, bf16[384,4096]{1,0:T(8,128)(2,1)S(1)} %get-tuple-element.7.in_k, bf16[384,4096]{1,0:T(8,128)(2,1)S(1)} %get-tuple-element.8.in_v), custom_call_target="tpu_custom_call" | custom-call | tf_op jit(solution)/shard_map/pallas_call | solution.py:448
